TPU v7x, 256 devices: a whole 4x4x8 slice. The times are simulated.
256 devices in a mesh: tm: 8 (over x, core), cohort: 32 (over z, y).
Axes of the slice: x: 4, y: 4, z: 8, core: 2. Of those that a mesh axis runs over, the one named last changes fastest.
Arguments:
- transition: float32 [64, 64, 256, 256], P('tm', 'cohort'), may hold values from 0 to 1, as said below
- entry: int32 [64], P('cohort'), may hold values from 0 to 63, as said below
- share: float32 [64], P('cohort'), may hold values from 0.1 to 1
Outputs:
- cumulative: float32 [64, 64, 256, 256], P('tm', 'cohort')
- pooled: float32 [64, 256, 256], P('tm', 'cohort')
Inputs may be any that keep to these rules, and one draw needn't show every extreme that they name: `entry`: month numbers within the window; some group enters at month 0 and some at the window's last month. `transition`: each row of every monthly matrix is nonnegative and sums to one, with a diagonal entry of at least 0.7.
All inputs are finite; a program needn't handle non-finite values.
Results may differ from a plain program's by a relative error of at most 0.0001.
Values sent between devices are 32-bit elements; how exact they have to be, the bound alone decides.
A program may use at most 64 MiB of HBM per device.

v0:
```python
import jax
import jax.numpy as jnp
from jax import lax
from jax.sharding import PartitionSpec as P

kernel_weights = (1.0 / 16, 2.0 / 16, 3.0 / 16, 4.0 / 16, 3.0 / 16, 2.0 / 16, 1.0 / 16)


def with_halo(block, sides, width):
    for axis, dim in sides:
        count = lax.axis_size(axis)
        forward = [(i, i + 1) for i in range(count - 1)]
        backward = [(target, source) for source, target in forward]
        low = lax.ppermute(
            lax.slice_in_dim(block, block.shape[dim] - width, None, axis=dim), axis, forward
        )
        high = lax.ppermute(lax.slice_in_dim(block, 0, width, axis=dim), axis, backward)
        block = jnp.concatenate([low, block, high], axis=dim)
    return block


def shifted(array, axis, by):
    peers = lax.axis_size(axis)
    pairs = [(i, i + by) for i in range(peers) if 0 <= i + by < peers]
    return lax.ppermute(array, axis, pairs)


def chain_product(earlier, later):
    return jnp.einsum("gij,gjk->gik", earlier, later, precision=lax.Precision.HIGHEST)


def on_device(transition, entry, share):
    months_dev = transition.shape[0]
    states = transition.shape[2]
    months_all = months_dev * lax.axis_size("tm")
    padded = with_halo(transition, (("tm", 0),), 3)
    first_month = lax.axis_index("tm") * months_dev
    month_idx = first_month + jnp.arange(months_dev)
    smoothed = jnp.zeros_like(transition)
    weight_sum = jnp.zeros((months_dev,), transition.dtype)
    for offset in range(7):
        smoothed = smoothed + kernel_weights[offset] * padded[offset : offset + months_dev]
        inside = (month_idx + offset - 3 >= 0) & (month_idx + offset - 3 < months_all)
        weight_sum = weight_sum + jnp.where(inside, kernel_weights[offset], 0.0).astype(
            transition.dtype
        )
    graduated = smoothed / weight_sum[:, None, None, None]
    unit = jnp.eye(states, dtype=transition.dtype)
    active = month_idx[:, None] >= entry[None, :]
    monthly = jnp.where(active[:, :, None, None], graduated, unit)

    def advance(running, matrix):
        nxt = chain_product(running, matrix)
        return (nxt, nxt)

    start_state = jnp.broadcast_to(unit, transition.shape[1:])
    block_total, prefix = lax.scan(advance, start_state, monthly)
    is_first = lax.axis_index("tm") == 0

    def pass_once(step, running):
        received = shifted(chain_product(running, block_total), "tm", 1)
        return jnp.where(is_first, start_state, received)

    incoming = lax.fori_loop(0, lax.axis_size("tm") - 1, pass_once, start_state)
    cumulative = jnp.einsum("gij,mgjk->mgik", incoming, prefix, precision=lax.Precision.HIGHEST)
    weighted = jnp.einsum("g,mgij->mij", share, cumulative, precision=lax.Precision.HIGHEST)
    pooled = lax.psum_scatter(weighted, "cohort", scatter_dimension=1, tiled=True)
    return (cumulative, pooled)


def solution(mesh):
    placed = (P("tm", "cohort", None, None), P("cohort"), P("cohort"))
    return jax.shard_map(
        on_device,
        mesh=mesh,
        in_specs=placed,
        out_specs=(P("tm", "cohort", None, None), P("tm", "cohort", None)),
        check_vma=False,
    )
```

profile of v0, /device:TPU:6, one launch (start us, length us, event | category | flops | bytes accessed | tf_op | source)
XLA Modules:
  0.0 411.3 jit_solution(2797861657724601192)
XLA Ops:
  7.2 0.0 copy-start
  7.2 0.0 reduce-scatter.2.cloned.1.call-start
  7.2 5.4 %copy.6 = f32[8,2,256,256]{2,3,1,0:T(8,128)} copy(f32[8,2,256,256]{3,2,1,0:T(8,128)} %param.7) | data formatting | bytes 8388608 | tf_op args[0]
  12.6 0.0 copy-start.1
  12.6 3.7 fusion.34
  16.3 1.9 collective-permute-start.1
  18.3 3.6 collective-permute-start.2
  22.0 0.1 copy.24
  22.1 0.0 copy-done.1
  22.1 0.1 broadcast_compare_fusion
  22.2 16.1 %collective-permute-done.1 = f32[3,2,256,256]{2,3,1,0:T(8,128)S(1)} collective-permute-done((f32[3,2,256,256]{2,3,1,0:T(8,128)}, f32[3,2,256,256]{2,3,1,0:T(8,128)S(1)}, u32[]{:S(2)}, u32[]{:S(2)}) %collective-permute-start.1) | collective-permute-done | bytes 1572896 | tf_op jit(solution)/shard_map/ppermute | solution.py:14
  38.3 1.9 collective-permute-done.2
  40.1 12.8 %fusion.11 = f32[8,2,256,256]{2,3,1,0:T(8,128)} fusion(f32[8,2,256,256]{2,3,1,0:T(8,128)} %copy.6, f32[3,2,256,256]{2,3,1,0:T(8,128)} %collective-permute-done.2, f32[3,2,256,256]{2,3,1,0:T(8,128)S(1)} %collective-permute-done.1, f32[256,256]{0,1:T(8,128)S(1)} %copy.24, f32[8]{0:T(128)S(1)} %fusion.31, pred[8,2]{1,0:T(8,128)(4,1)S(1)} %broadcast_compare_fusion), kind=kLoop, calls=%fused_computation.20 | loop fusion | flops 22020096 | bytes 11796528 | tf_op jit(solution)/shard_map/jit(_where)/select_n | solution.py:50
  53.0 20.3 %while.23 = (s32[]{:T(128)}, f32[2,256,256]{1,2,0:T(8,128)S(1)}, f32[8,2,256,256]{2,3,0,1:T(8,128)}, f32[8,2,256,256]{2,3,1,0:T(8,128)}, s32[]{:T(128)}) while((s32[]{:T(128)}, f32[2,256,256]{1,2,0:T(8,128)S(1)}, f32[8,2,256,256]{2,3,0,1:T(8,128)}, f32[8,2,256,256]{2,3,1,0:T(8,128)}, s32[]{:T(128)}) %tuple.45), condition=%wide.region_1.2_spmd, body=%wide.region_0.1_spmd.sunk | while | flops 402653184 | bytes 3146813 | solution.py:57
  53.1 2.5 bitcast_dynamic-update-slice_fusion.2
  55.6 2.5 bitcast_dynamic-update-slice_fusion.2
  58.1 2.5 bitcast_dynamic-update-slice_fusion.2
  60.7 2.5 bitcast_dynamic-update-slice_fusion.2
  63.2 2.5 bitcast_dynamic-update-slice_fusion.2
  65.8 2.5 bitcast_dynamic-update-slice_fusion.2
  68.3 2.5 bitcast_dynamic-update-slice_fusion.2
  70.8 2.5 bitcast_dynamic-update-slice_fusion.2
  73.3 0.2 copy.13
  73.6 78.9 %while.24 = (s32[]{:T(128)}, f32[2,256,256]{2,1,0:T(8,128)S(1)}, pred[]{:T(512)}, f32[2,256,256]{2,1,0:T(8,128)S(1)}, f32[256,256]{1,0:T(8,128)S(1)}, /*index=5*/s32[]{:T(128)}) while((s32[]{:T(128)}, f32[2,256,256]{2,1,0:T(8,128)S(1)}, pred[]{:T(512)}, f32[2,256,256]{2,1,0:T(8,128)S(1)}, f32[256,256]{1,0:T(8,128)S(1)}, ...), condition=%wide.region_3.4_spmd.clone, body=%wide.region_2.3_spmd.clone.sunk | while | flops 402784256 | bytes 4980846 | solution.py:64
  73.6 0.7 fusion.48
  74.2 1.9 collective-permute-start
  76.2 8.7 %collective-permute-done = f32[2,256,256]{2,1,0:T(8,128)S(1)} collective-permute-done((f32[2,256,256]{2,1,0:T(8,128)S(1)}, f32[2,256,256]{2,1,0:T(8,128)S(1)}, u32[]{:S(2)}, u32[]{:S(2)}) %collective-permute-start) | collective-permute-done | bytes 524320 | tf_op jit(solution)/shard_map/while/body/eval_jaxpr/ppermute | solution.py:25
  84.9 0.1 broadcast_select_fusion.2
  85.0 0.7 fusion.48
  85.7 1.9 collective-permute-start
  87.6 8.6 %collective-permute-done = f32[2,256,256]{2,1,0:T(8,128)S(1)} collective-permute-done((f32[2,256,256]{2,1,0:T(8,128)S(1)}, f32[2,256,256]{2,1,0:T(8,128)S(1)}, u32[]{:S(2)}, u32[]{:S(2)}) %collective-permute-start) | collective-permute-done | bytes 524320 | tf_op jit(solution)/shard_map/while/body/eval_jaxpr/ppermute | solution.py:25
  96.2 0.1 broadcast_select_fusion.2
  96.2 0.7 fusion.48
  96.9 1.9 collective-permute-start
  98.8 8.6 %collective-permute-done = f32[2,256,256]{2,1,0:T(8,128)S(1)} collective-permute-done((f32[2,256,256]{2,1,0:T(8,128)S(1)}, f32[2,256,256]{2,1,0:T(8,128)S(1)}, u32[]{:S(2)}, u32[]{:S(2)}) %collective-permute-start) | collective-permute-done | bytes 524320 | tf_op jit(solution)/shard_map/while/body/eval_jaxpr/ppermute | solution.py:25
  107.4 0.1 broadcast_select_fusion.2
  107.5 0.7 fusion.48
  108.1 1.9 collective-permute-start
  110.1 8.6 %collective-permute-done = f32[2,256,256]{2,1,0:T(8,128)S(1)} collective-permute-done((f32[2,256,256]{2,1,0:T(8,128)S(1)}, f32[2,256,256]{2,1,0:T(8,128)S(1)}, u32[]{:S(2)}, u32[]{:S(2)}) %collective-permute-start) | collective-permute-done | bytes 524320 | tf_op jit(solution)/shard_map/while/body/eval_jaxpr/ppermute | solution.py:25
  118.6 0.1 broadcast_select_fusion.2
  118.7 0.7 fusion.48
  119.4 1.9 collective-permute-start
  121.3 8.6 %collective-permute-done = f32[2,256,256]{2,1,0:T(8,128)S(1)} collective-permute-done((f32[2,256,256]{2,1,0:T(8,128)S(1)}, f32[2,256,256]{2,1,0:T(8,128)S(1)}, u32[]{:S(2)}, u32[]{:S(2)}) %collective-permute-start) | collective-permute-done | bytes 524320 | tf_op jit(solution)/shard_map/while/body/eval_jaxpr/ppermute | solution.py:25
  129.9 0.1 broadcast_select_fusion.2
  130.0 0.7 fusion.48
  130.6 1.9 collective-permute-start
  132.6 8.6 %collective-permute-done = f32[2,256,256]{2,1,0:T(8,128)S(1)} collective-permute-done((f32[2,256,256]{2,1,0:T(8,128)S(1)}, f32[2,256,256]{2,1,0:T(8,128)S(1)}, u32[]{:S(2)}, u32[]{:S(2)}) %collective-permute-start) | collective-permute-done | bytes 524320 | tf_op jit(solution)/shard_map/while/body/eval_jaxpr/ppermute | solution.py:25
  141.1 0.1 broadcast_select_fusion.2
  141.2 0.7 fusion.48
  141.9 1.9 collective-permute-start
  143.8 8.6 %collective-permute-done = f32[2,256,256]{2,1,0:T(8,128)S(1)} collective-permute-done((f32[2,256,256]{2,1,0:T(8,128)S(1)}, f32[2,256,256]{2,1,0:T(8,128)S(1)}, u32[]{:S(2)}, u32[]{:S(2)}) %collective-permute-start) | collective-permute-done | bytes 524320 | tf_op jit(solution)/shard_map/while/body/eval_jaxpr/ppermute | solution.py:25
  152.4 0.1 broadcast_select_fusion.2
  152.4 7.8 %convolution_bitcast_fusion = f32[8,2,256,256]{2,3,0,1:T(8,128)} fusion(f32[8,2,256,256]{2,3,0,1:T(8,128)} %get-tuple-element.52, f32[2,256,256]{2,1,0:T(8,128)S(1)} %get-tuple-element.54), kind=kOutput, calls=%fused_computation.35 | convolution fusion | flops 3221225472 | bytes 8912896 | tf_op jit(solution)/shard_map/gij,mgjk->mgik/dot_general | solution.py:65
  160.2 7.2 %copy.18 = f32[8,2,256,256]{3,1,2,0:T(2,128)} copy(f32[8,2,256,256]{2,3,0,1:T(8,128)} %convolution_bitcast_fusion) | data formatting | bytes 8388608 | tf_op jit(solution)/shard_map/gij,mgjk->mgik/transpose | solution.py:65
  167.5 0.0 copy-done
  167.5 16.3 %fusion.32 = f32[1,8,256,256]{3,0,2,1:T(1,128)S(1)} fusion(f32[8,2,256,256]{3,1,2,0:T(2,128)} %copy.18, f32[2]{0:T(128)S(1)} %copy-done), kind=kOutput, calls=%fused_computation.55 | convolution fusion | flops 12582912 | bytes 6291464 | tf_op jit(solution)/shard_map/g,mgij->mij/dot_general | solution.py:66
  183.8 1.5 copy.26
  185.3 0.0 reduce-scatter.2.cloned.1.call-update
  185.3 5.4 %copy.15 = f32[8,2,256,256]{3,2,1,0:T(8,128)} copy(f32[8,2,256,256]{2,3,0,1:T(8,128)} %convolution_bitcast_fusion) | data formatting | bytes 8388608
  190.7 213.8 %reduce-scatter.2.cloned.1.call-done = f32[8,8,256]{2,1,0:T(8,128)} async-done(((f32[8,256,256]{2,1,0:T(8,128)}), f32[8,8,256]{2,1,0:T(8,128)}) %reduce-scatter.2.cloned.1.call-update) | async-done | bytes 65552 | tf_op jit(solution)/shard_map/reduce_scatter | solution.py:67
  (14 shorter events, 0.4 us)
Async XLA Ops:
  7.2 160.3 %copy-start = (f32[2]{0:T(128)S(1)}, f32[2]{0:T(128)}, u32[]{:S(2)}) copy-start(f32[2]{0:T(128)} %param.9) | copy-start | bytes 28
  7.2 397.3 %reduce-scatter.2.cloned.1.call-start = ((), (), s32[]{:S(2)}) async-start(), calls=%async_computation.1 | async-start | bytes 2162688 | tf_op jit(solution)/shard_map/reduce_scatter | solution.py:67
  12.6 9.5 %copy-start.1 = (s32[2]{0:T(128)S(1)}, s32[2]{0:T(128)}, u32[]{:S(2)}) copy-start(s32[2]{0:T(128)} %param.8) | copy-start | bytes 28
  16.3 21.9 %collective-permute-start.1 = (f32[3,2,256,256]{2,3,1,0:T(8,128)}, f32[3,2,256,256]{2,3,1,0:T(8,128)S(1)}, u32[]{:S(2)}, u32[]{:S(2)}) collective-permute-start(f32[3,2,256,256]{2,3,1,0:T(8,128)} %get-tuple-element.99), channel_id=1, source_target_pairs={{0,32},{32,64},{64,96},{96,128},{128,160},{160,192},{192,224},{1,3... | collective-permute-start | bytes 4718600 | tf_op jit(solution)/shard_map/ppermute | solution.py:14
  18.3 21.9 %collective-permute-start.2 = (f32[3,2,256,256]{2,3,1,0:T(8,128)}, f32[3,2,256,256]{2,3,1,0:T(8,128)}, u32[]{:S(2)}, u32[]{:S(2)}) collective-permute-start(f32[3,2,256,256]{2,3,1,0:T(8,128)} %get-tuple-element.100), channel_id=1, source_target_pairs={{32,0},{64,32},{96,64},{128,96},{160,128},{192,160},{224,192},{33,... | collective-permute-start | bytes 4718600 | tf_op jit(solution)/shard_map/ppermute | solution.py:17
  74.2 10.7 %collective-permute-start = (f32[2,256,256]{2,1,0:T(8,128)S(1)}, f32[2,256,256]{2,1,0:T(8,128)S(1)}, u32[]{:S(2)}, u32[]{:S(2)}) collective-permute-start(f32[2,256,256]{2,1,0:T(8,128)S(1)} %fusion.48), channel_id=1, source_target_pairs={{0,32},{32,64},{64,96},{96,128},{128,160},{160,192},{192,224},{1,3... | collective-permute-start | bytes 1572872 | tf_op jit(solution)/shard_map/while/body/eval_jaxpr/ppermute | solution.py:25
  85.7 10.5 %collective-permute-start = (f32[2,256,256]{2,1,0:T(8,128)S(1)}, f32[2,256,256]{2,1,0:T(8,128)S(1)}, u32[]{:S(2)}, u32[]{:S(2)}) collective-permute-start(f32[2,256,256]{2,1,0:T(8,128)S(1)} %fusion.48), channel_id=1, source_target_pairs={{0,32},{32,64},{64,96},{96,128},{128,160},{160,192},{192,224},{1,3... | collective-permute-start | bytes 1572872 | tf_op jit(solution)/shard_map/while/body/eval_jaxpr/ppermute | solution.py:25
  96.9 10.5 %collective-permute-start = (f32[2,256,256]{2,1,0:T(8,128)S(1)}, f32[2,256,256]{2,1,0:T(8,128)S(1)}, u32[]{:S(2)}, u32[]{:S(2)}) collective-permute-start(f32[2,256,256]{2,1,0:T(8,128)S(1)} %fusion.48), channel_id=1, source_target_pairs={{0,32},{32,64},{64,96},{96,128},{128,160},{160,192},{192,224},{1,3... | collective-permute-start | bytes 1572872 | tf_op jit(solution)/shard_map/while/body/eval_jaxpr/ppermute | solution.py:25
  108.1 10.5 %collective-permute-start = (f32[2,256,256]{2,1,0:T(8,128)S(1)}, f32[2,256,256]{2,1,0:T(8,128)S(1)}, u32[]{:S(2)}, u32[]{:S(2)}) collective-permute-start(f32[2,256,256]{2,1,0:T(8,128)S(1)} %fusion.48), channel_id=1, source_target_pairs={{0,32},{32,64},{64,96},{96,128},{128,160},{160,192},{192,224},{1,3... | collective-permute-start | bytes 1572872 | tf_op jit(solution)/shard_map/while/body/eval_jaxpr/ppermute | solution.py:25
  119.4 10.5 %collective-permute-start = (f32[2,256,256]{2,1,0:T(8,128)S(1)}, f32[2,256,256]{2,1,0:T(8,128)S(1)}, u32[]{:S(2)}, u32[]{:S(2)}) collective-permute-start(f32[2,256,256]{2,1,0:T(8,128)S(1)} %fusion.48), channel_id=1, source_target_pairs={{0,32},{32,64},{64,96},{96,128},{128,160},{160,192},{192,224},{1,3... | collective-permute-start | bytes 1572872 | tf_op jit(solution)/shard_map/while/body/eval_jaxpr/ppermute | solution.py:25
  130.6 10.5 %collective-permute-start = (f32[2,256,256]{2,1,0:T(8,128)S(1)}, f32[2,256,256]{2,1,0:T(8,128)S(1)}, u32[]{:S(2)}, u32[]{:S(2)}) collective-permute-start(f32[2,256,256]{2,1,0:T(8,128)S(1)} %fusion.48), channel_id=1, source_target_pairs={{0,32},{32,64},{64,96},{96,128},{128,160},{160,192},{192,224},{1,3... | collective-permute-start | bytes 1572872 | tf_op jit(solution)/shard_map/while/body/eval_jaxpr/ppermute | solution.py:25
  141.9 10.5 %collective-permute-start = (f32[2,256,256]{2,1,0:T(8,128)S(1)}, f32[2,256,256]{2,1,0:T(8,128)S(1)}, u32[]{:S(2)}, u32[]{:S(2)}) collective-permute-start(f32[2,256,256]{2,1,0:T(8,128)S(1)} %fusion.48), channel_id=1, source_target_pairs={{0,32},{32,64},{64,96},{96,128},{128,160},{160,192},{192,224},{1,3... | collective-permute-start | bytes 1572872 | tf_op jit(solution)/shard_map/while/body/eval_jaxpr/ppermute | solution.py:25
Sparse Core Ops, SparseCore 0:
  185.4 219.0 reduce-scatter.1
where the time goes:
time: 412 us; the launch traced here: 411 us
  waiting for transfers between devices  292 us (71%)
  matrix products  48.7 us (12%)
  local copies, waits for them, and re-layouts  23.9 us (6%)
  starting transfers between devices  19 us (5%)
  between operations  14.1 us (3%)
  other arithmetic  13.3 us (3%)
    reduce_scatter x1, waiting for transfers between devices, on_device(): lax.psum_scatter(weighted, 'cohort', scatter_dimension=1, tiled=True)  214 us
    ppermute x7, waiting for transfers between devices, shifted(): return lax.ppermute(array, axis, pairs)  60.2 us
    dot_general x15, matrix products, chain_product(): jnp.einsum('gij,gjk->gik', earlier, later, precision=lax.Precision.HIGHEST)  24.6 us
    dot_general x1, matrix products, on_device(): jnp.einsum('g,mgij->mij', share, cumulative, precision=lax.Precision.HIGH...  16.3 us
    ppermute x1, waiting for transfers between devices, with_halo(): lax.ppermute(lax.slice_in_dim(block, block.shape[dim] - width, None, axis...  16.1 us
    ppermute x7, starting transfers between devices, shifted(): return lax.ppermute(array, axis, pairs)  13.4 us
    select_n x1, other arithmetic, on_device(): monthly = jnp.where(active[:, :, None, None], graduated, unit)  12.8 us
    unnamed x8, local copies, waits for them, and re-layouts  11.1 us
  transfers between devices with their start and end apart: 10, of which 10 were waited for; matrix products, arithmetic and copies ran while one was open for 1% of the time, Pallas kernels for 0%

commit v1 on v0

v1 whole, which is shorter than its diff:
```python
import functools

import jax
import jax.numpy as jnp
from jax import lax
from jax.experimental import pallas as pl
from jax.experimental.pallas import tpu as pltpu
from jax.sharding import PartitionSpec as P

MESH = pl.DeviceIdType.MESH
F32 = jnp.float32
BF16 = jnp.bfloat16
VMEM_LIMIT = 56 * 1024 * 1024


def ring_places(nz):
    half = nz // 2
    plus = [(p, 0) for p in range(half)] + [(p, 1) for p in range(half - 2, -1, -1)]
    minus = [(p, 1) for p in range(half - 1)] + [(half - 1, 0)] + [(p, 0) for p in range(half - 2, -1, -1)]
    return plus, minus


def kernel(
    nz, ny, trans, entry, share, cum_out, pooled,
    own, hp, hn, mon, pre, t0s, t0r, t0b, carry, cab, cum, wa, wb, ra, rb, rya, ryb,
    own_sem, fs_sem, bs_sem, hp_sem, hn_sem, t0_sem, cs_sem, cr_sem, cf_sem, out_sem,
    as_sem, ar_sem, bzs_sem, bzr_sem, yas_sem, yar_sem, ybs_sem, ybr_sem,
):
    n = own.shape[-1]
    pairs = nz // 2
    rows = n // nz
    sub = rows // ny
    block = 2 * rows
    tm = lax.axis_index("tm")
    co = lax.axis_index("cohort")
    ntm = lax.axis_size("tm")
    core, chip = lax.rem(tm, 2), tm // 2
    z, y = co // ny, lax.rem(co, ny)
    has_prev, has_next = tm > 0, tm < ntm - 1
    first_chip, last_chip = chip == 0, chip == ntm // 2 - 1
    z_up = lax.rem(z + 1, nz) * ny + y
    z_down = lax.rem(z + nz - 1, nz) * ny + y

    def y_peer(o):
        return lax.rem(y + o, ny)

    barrier = pltpu.get_barrier_semaphore()

    def greet(t, c):
        pl.semaphore_signal(barrier, inc=1, device_id=(t, c), device_id_type=MESH)

    near = (
        (has_prev, tm - 1), (has_next, tm + 1),
        ((core == 1) & (tm > 1), tm - 2), ((core == 1) & (tm < ntm - 2), tm + 2),
    )
    peers = 1 + ny
    for cond, t in near:
        pl.when(cond)(functools.partial(greet, t, co))
        peers = peers + jnp.where(cond, 1, 0)
    for c in [z_up, z_down] + [z * ny + y_peer(o) for o in range(1, ny)]:
        greet(tm, c)
    pl.semaphore_wait(barrier, peers)

    def remote(src, dst, ss, rs, t, c):
        return pltpu.make_async_remote_copy(
            src_ref=src, dst_ref=dst, send_sem=ss, recv_sem=rs, device_id=(t, c), device_id_type=MESH
        )

    def fwd_halo(i):
        return remote(trans.at[5 + i], hp.at[i], fs_sem.at[i], hp_sem.at[i], tm + 1, co)

    def bwd_halo(i):
        return remote(trans.at[i], hn.at[i], bs_sem.at[i], hn_sem.at[i], tm - 1, co)

    def own_copy(i):
        return pltpu.make_async_copy(trans.at[i], own.at[i], own_sem.at[i])

    @pl.when(has_next)
    def _():
        for i in (2, 1, 0):
            fwd_halo(i).start()

    @pl.when(has_prev)
    def _():
        for i in (0, 1, 2):
            bwd_halo(i).start()

    for i in range(8):
        own_copy(i).start()

    @pl.when(jnp.logical_not(has_prev))
    def _():
        hp[...] = jnp.zeros_like(hp)

    @pl.when(jnp.logical_not(has_next))
    def _():
        hn[...] = jnp.zeros_like(hn)

    strip = min(64, n)

    def graduate(t):
        def at(e):
            return (hp, e + 3) if e < 0 else ((hn, e - 8) if e > 7 else (own, e))

        edge = {0: 10, 1: 13, 2: 15, 5: 15, 6: 13, 7: 10}.get(t)
        scale = 1.0 / 16
        if edge is not None:
            scale = jnp.where(tm == (0 if t < 3 else ntm - 1), F32(1.0 / edge), F32(1.0 / 16))

        def step(i, _):
            g, r0 = i // (n // strip), pl.multiple_of(lax.rem(i, n // strip) * strip, strip)
            act = jnp.where(8 * tm + t >= entry[g], F32(1.0), F32(0.0))

            def load(e):
                ref, k = at(e)
                return ref[k, g, pl.ds(r0, strip), :]

            total = (
                4.0 * load(t) + 3.0 * (load(t - 1) + load(t + 1))
                + 2.0 * (load(t - 2) + load(t + 2)) + (load(t - 3) + load(t + 3))
            )
            row = lax.broadcasted_iota(jnp.int32, (strip, n), 0) + r0
            col = lax.broadcasted_iota(jnp.int32, (strip, n), 1)
            unit = jnp.where(row == col, 1.0 - act, 0.0)
            v = total * (act * scale) + unit
            hi = v.astype(BF16)
            mon[t, g, 0, pl.ds(r0, strip), :] = hi
            mon[t, g, 1, pl.ds(r0, strip), :] = (v - hi.astype(F32)).astype(BF16)
            return 0

        lax.fori_loop(0, 2 * (n // strip), step, 0)

    def dot(a, b):
        return jnp.dot(a, b, preferred_element_type=F32)

    def times(a, b):
        r = a.shape[1]
        both = dot(a.reshape(2 * r, n), b[0])
        return both[:r] + both[r:] + dot(a[0], b[1])

    def halves(ref, v):
        hi = v.astype(BF16)
        ref[0] = hi
        ref[1] = (v - hi.astype(F32)).astype(BF16)

    def multiply(dst, a, b, keep=None):
        def step(g, _):
            v = times(a(g), b(g))
            halves(pre.at[dst, g], v)
            if keep is not None:
                keep[g] = v
            return 0
        lax.fori_loop(0, 2, step, 0)

    def take(ref, k):
        return lambda g: ref[k, g]

    def copy_pre(t):
        pre[t] = mon[t]

    def fwd_wait(i):
        pl.when(has_prev)(lambda: fwd_halo(i).wait_recv())

    def bwd_wait(i):
        pl.when(has_next)(lambda: bwd_halo(i).wait_recv())

    for i in range(8):
        own_copy(i).wait()
    graduate(3)
    graduate(4)

    def send_t0():
        return remote(t0s, t0r, t0_sem.at[0], t0_sem.at[1], tm + 1, co)

    @pl.when(core == 0)
    def _():
        for i in range(3):
            bwd_wait(i)
            graduate(5 + i)
        copy_pre(3)
        for t in range(4, 8):
            multiply(t, take(pre, t - 1), take(mon, t))
        fwd_wait(2)
        graduate(2)
        fwd_wait(1)
        graduate(1)
        copy_pre(1)
        multiply(2, take(mon, 1), take(mon, 2))
        for t in range(3, 8):
            multiply(t, take(pre, 2), take(pre, t))
        fwd_wait(0)
        graduate(0)
        multiply(7, take(mon, 0), take(pre, 7), t0s)
        send_t0().start()
        for t in range(6, 0, -1):
            multiply(t, take(mon, 0), take(pre, t))
        copy_pre(0)

    @pl.when(core == 1)
    def _():
        for i in (2, 1, 0):
            fwd_wait(i)
            graduate(i)
        copy_pre(0)
        for t in range(1, 5):
            multiply(t, take(pre, t - 1), take(mon, t))
        for t in range(5, 8):
            bwd_wait(t - 5)
            graduate(t)
            multiply(t, take(pre, t - 1), take(mon, t))
        send_t0().wait_recv()
        for g in range(2):
            halves(t0b.at[g], t0r[g])
        for t in range(7, -1, -1):
            multiply(t, lambda g: t0b[g], take(pre, t))

    def chunk(p, side):
        if p == pairs - 1:
            return lax.rem(z + nz - pairs, nz) if side == 0 else z
        return lax.rem(z + nz - 1 - p, nz) if side == 0 else lax.rem(z + 1 + p, nz)

    def carry_on(p):
        return remote(cum.at[p, 7], carry.at[p], cs_sem.at[p], cr_sem.at[p], tm + 2, co)

    def carry_back(p):
        return remote(carry.at[p], carry.at[p], cf_sem.at[p], cr_sem.at[p], tm - 1, co)

    def out_copy(p, side):
        return pltpu.make_async_copy(
            cum.at[p, :, :, pl.ds(side * rows, rows), :],
            cum_out.at[:, :, pl.ds(pl.multiple_of(chunk(p, side) * rows, rows), rows), :],
            out_sem.at[p, side],
        )

    def advance(p, t):
        total = None
        for g in range(2):
            v = times(cab[g], pre[t, g])
            cum[p, t, g] = v
            w = share[g] * v
            total = w if total is None else total + w
        return total

    plus, minus = ring_places(nz)
    places = (plus, minus)
    targets = (z_up, z_down)

    def a_copy(d, s):
        p, side = places[d][s]
        src = wa.at[p, pl.ds(2 * d, 2), pl.ds(side * rows, rows), :] if s == 0 else ra.at[d, s - 1]
        return remote(src, ra.at[d, s], as_sem.at[d, s], ar_sem.at[d, s], tm, targets[d])

    def a_step(d, s):
        p, side = places[d][s]
        if s > 0:
            a_copy(d, s - 1).wait_recv()
            ra[d, s - 1] += wa[p, 2 * d : 2 * d + 2, side * rows : (side + 1) * rows, :]
        a_copy(d, s).start()

    def yb_copy(p, side, o):
        src = wb.at[p, :, pl.ds(pl.multiple_of(side * rows + y_peer(o) * sub, sub), sub), :]
        k = 2 * p + side
        return remote(
            src, ryb.at[k, o - 1], ybs_sem.at[k, o - 1], ybr_sem.at[k, o - 1], tm, z * ny + y_peer(o)
        )

    def yb_sum(d, p, side):
        v = wb[p, 2 * d : 2 * d + 2, pl.ds(pl.multiple_of(side * rows + y * sub, sub), sub), :]
        for o in range(1, ny):
            v = v + ryb[2 * p + side, o - 1, 2 * d : 2 * d + 2]
        return v

    got = set()

    def yb_wait(p, side):
        if (p, side) not in got:
            got.add((p, side))
            for o in range(1, ny):
                yb_copy(p, side, o).wait_recv()

    def b_copy(d, s):
        return remote(rb.at[d, s], rb.at[d, s + 1], bzs_sem.at[d, s], bzr_sem.at[d, s], tm, targets[d])

    def b_step(d, s):
        p, side = places[d][s]
        yb_wait(p, side)
        v = yb_sum(d, p, side)
        if s > 0:
            b_copy(d, s - 1).wait_recv()
            rb[d, s] += v
        else:
            rb[d, 0] = v
        b_copy(d, s).start()

    for p in range(pairs):
        @pl.when(first_chip)
        def _():
            row = lax.broadcasted_iota(jnp.int32, (rows, n), 0)
            col = lax.broadcasted_iota(jnp.int32, (rows, n), 1)
            for side in range(2):
                unit = jnp.where(row + chunk(p, side) * rows == col, F32(1.0), F32(0.0))
                for g in range(2):
                    carry[p, g, side * rows : (side + 1) * rows, :] = unit

        @pl.when(jnp.logical_not(first_chip) & (core == 1))
        def _():
            carry_on(p).wait_recv()
            carry_back(p).start()

        @pl.when(jnp.logical_not(first_chip) & (core == 0))
        def _():
            carry_back(p).wait_recv()

        for g in range(2):
            halves(cab.at[g], carry[p, g])
        wb[p, 3] = advance(p, 7)
        pl.when((core == 1) & jnp.logical_not(last_chip))(lambda: carry_on(p).start())

        def b_month(t, _):
            wb[p, t] = advance(p, t + 4)
            return 0

        lax.fori_loop(0, 3, b_month, 0)
        for side in range(2):
            for o in range(1, ny):
                yb_copy(p, side, o).start()

        def a_month(t, _):
            wa[p, t] = advance(p, t)
            return 0

        lax.fori_loop(0, 4, a_month, 0)
        for side in range(2):
            out_copy(p, side).start()
        for d in range(2):
            a_step(d, p)
        if p > 0:
            for d in range(2):
                b_step(d, p - 1)

    last = (pairs - 1, 1)
    for s in range(pairs, nz - 1):
        for d in range(2):
            a_step(d, s)
        for d in range(2):
            b_step(d, s - 1)

    for d in range(2):
        a_copy(d, nz - 2).wait_recv()
        ra[d, nz - 2] += wa[last[0], 2 * d : 2 * d + 2, rows : 2 * rows, :]

    def ya_copy(d, o):
        src = ra.at[d, nz - 2, :, pl.ds(pl.multiple_of(y_peer(o) * sub, sub), sub), :]
        return remote(
            src, rya.at[d, o - 1], yas_sem.at[d, o - 1], yar_sem.at[d, o - 1], tm, z * ny + y_peer(o)
        )

    for d in range(2):
        for o in range(1, ny):
            ya_copy(d, o).start()
    for d in range(2):
        b_step(d, nz - 2)
    yb_wait(*last)
    for d in range(2):
        v = yb_sum(d, *last)
        b_copy(d, nz - 2).wait_recv()
        pooled[4 + 2 * d : 6 + 2 * d] = v + rb[d, nz - 1]
    for d in range(2):
        v = ra[d, nz - 2, :, pl.ds(pl.multiple_of(y * sub, sub), sub), :]
        for o in range(1, ny):
            ya_copy(d, o).wait_recv()
            v = v + rya[d, o - 1]
        pooled[2 * d : 2 * d + 2] = v

    for i in range(3):
        pl.when(has_next)(lambda: fwd_halo(i).wait_send())
        pl.when(has_prev)(lambda: bwd_halo(i).wait_send())
    pl.when(core == 0)(lambda: send_t0().wait_send())
    for p in range(pairs):
        pl.when((core == 1) & jnp.logical_not(last_chip))(lambda: carry_on(p).wait_send())
        pl.when((core == 1) & jnp.logical_not(first_chip))(lambda: carry_back(p).wait_send())
        for side in range(2):
            out_copy(p, side).wait()
            for o in range(1, ny):
                yb_copy(p, side, o).wait_send()
    for d in range(2):
        for s in range(nz - 1):
            a_copy(d, s).wait_send()
            b_copy(d, s).wait_send()
        for o in range(1, ny):
            ya_copy(d, o).wait_send()


def on_device(nz, ny, transition, entry, share):
    n = transition.shape[-1]
    pairs, rows = nz // 2, n // nz
    sub = rows // ny
    dma = pltpu.SemaphoreType.DMA
    return pl.pallas_call(
        functools.partial(kernel, nz, ny),
        out_shape=(
            jax.ShapeDtypeStruct(transition.shape, F32),
            jax.ShapeDtypeStruct((8, sub, n), F32),
        ),
        in_specs=[
            pl.BlockSpec(memory_space=pl.ANY),
            pl.BlockSpec(memory_space=pltpu.SMEM),
            pl.BlockSpec(memory_space=pltpu.SMEM),
        ],
        out_specs=(pl.BlockSpec(memory_space=pl.ANY), pl.BlockSpec(memory_space=pltpu.VMEM)),
        scratch_shapes=[
            pltpu.VMEM((8, 2, n, n), F32),
            pltpu.VMEM((3, 2, n, n), F32),
            pltpu.VMEM((3, 2, n, n), F32),
            pltpu.VMEM((8, 2, 2, n, n), BF16),
            pltpu.VMEM((8, 2, 2, n, n), BF16),
            pltpu.VMEM((2, n, n), F32),
            pltpu.VMEM((2, n, n), F32),
            pltpu.VMEM((2, 2, n, n), BF16),
            pltpu.VMEM((pairs, 2, 2 * rows, n), F32),
            pltpu.VMEM((2, 2, 2 * rows, n), BF16),
            pltpu.VMEM((pairs, 8, 2, 2 * rows, n), F32),
            pltpu.VMEM((pairs, 4, 2 * rows, n), F32),
            pltpu.VMEM((pairs, 4, 2 * rows, n), F32),
            pltpu.VMEM((2, nz - 1, 2, rows, n), F32),
            pltpu.VMEM((2, nz, 2, sub, n), F32),
            pltpu.VMEM((2, ny - 1, 2, sub, n), F32),
            pltpu.VMEM((nz, ny - 1, 4, sub, n), F32),
            dma((8,)), dma((3,)), dma((3,)), dma((3,)), dma((3,)), dma((2,)),
            dma((pairs,)), dma((pairs,)), dma((pairs,)), dma((pairs, 2)),
            dma((2, nz - 1)), dma((2, nz - 1)), dma((2, nz - 1)), dma((2, nz - 1)),
            dma((2, ny - 1)), dma((2, ny - 1)), dma((nz, ny - 1)), dma((nz, ny - 1)),
        ],
        compiler_params=pltpu.CompilerParams(
            collective_id=0, has_side_effects=True, vmem_limit_bytes=VMEM_LIMIT
        ),
        cost_estimate=pl.CostEstimate(
            flops=3 * 2 * 46 * n**3, bytes_accessed=2 * 4 * 16 * n * n, transcendentals=0
        ),
    )(transition, entry, share)


def solution(mesh, nz=8, ny=4):
    return jax.shard_map(
        functools.partial(on_device, nz, ny),
        mesh=mesh,
        in_specs=(P("tm", "cohort", None, None), P("cohort"), P("cohort")),
        out_specs=(P("tm", "cohort", None, None), P("tm", "cohort", None)),
        check_vma=False,
    )
```

time: 412 us -> 83.3 us (0.20)
  waiting for transfers between devices: 292 us -> 0 us
  Pallas kernels: 0 us -> 77.3 us
  matrix products: 48.7 us -> 0 us
  starting transfers between devices: 19 us -> 0 us
  local copies, waits for them, and re-layouts: 23.9 us -> 5.26 us
  between operations: 14.1 us -> 0.65 us
  other arithmetic: 13.3 us -> 0 us
    reduce_scatter x1 -> x0, waiting for transfers between devices: 214 us -> none  [on_device(): lax.psum_scatter(weighted, 'cohort', scatter_dimension=1, tiled=True)]
    ppermute x9 -> x0, waiting for transfers between devices: 78.1 us -> none  [the longest x7 60.2 us: shifted(): return lax.ppermute(array, axis, pairs)]
    pallas_call x0 -> x1, Pallas kernels: none -> 77.3 us  [on_device(): pl.pallas_call(functools.partial(kernel, nz, ny), out_shape=(jax.ShapeDty...]
    dot_general x17 -> x0, matrix products: 48.7 us -> none  [the longest x15 24.6 us: chain_product(): jnp.einsum('gij,gjk->gik', earlier, later, precision=lax.Precision.HIGHEST)]
    ppermute x9 -> x0, starting transfers between devices: 19 us -> none  [the longest x7 13.4 us: shifted(): return lax.ppermute(array, axis, pairs)]
    select_n x8 -> x0, other arithmetic: 13.2 us -> none  [the longest x1 12.8 us: on_device(): monthly = jnp.where(active[:, :, None, None], graduated, unit)]
    transpose x1 -> x0, local copies, waits for them, and re-layouts: 7.22 us -> none  [on_device(): jnp.einsum('gij,mgjk->mgik', incoming, prefix, precision=lax.Precision.HI...]
    unnamed x8 -> x4, local copies, waits for them, and re-layouts: 11.1 us -> 5.26 us
  transfers between devices with their start and end apart: 10 -> 0, of which waited for: 10 -> 0; matrix products, arithmetic and copies ran while one was open for 1% -> 0% of each run, Pallas kernels for 0% -> 0%
where the time goes in v1:
time: 83.3 us; the launch traced here: 83.2 us
  Pallas kernels  77.3 us (93%)
  local copies, waits for them, and re-layouts  5.26 us (6%)
    pallas_call x1, Pallas kernels, on_device(): pl.pallas_call(functools.partial(kernel, nz, ny), out_shape=(jax.ShapeDty...  77.3 us
    unnamed x4, local copies, waits for them, and re-layouts  5.26 us

profile of v1, /device:TPU:6, one launch (start us, length us, event | category | flops | bytes accessed | tf_op | source)
XLA Modules:
  0.0 83.2 jit_solution(4651076191668642840)
XLA Ops:
  0.6 77.3 %shard_map.50 = (f32[8,2,256,256]{3,2,1,0:T(8,128)}, f32[8,8,256]{2,1,0:T(8,128)}) custom-call(f32[8,2,256,256]{3,2,1,0:T(8,128)} %trans.1, s32[2]{0:T(128)} %entry.1, f32[2]{0:T(128)} %share.1), custom_call_target="tpu_custom_call" | custom-call | flops 4630511616 | bytes 8388608 | tf_op jit(solution)/shard_map/pallas_call | solution.py:399
  77.9 0.0 copy-start
  77.9 4.6 %copy.7 = f32[8,2,256,256]{3,2,1,0:T(8,128)} copy(f32[8,2,256,256]{3,2,1,0:T(8,128)} %get-tuple-element.4) | data formatting | bytes 8388608
  82.5 0.0 copy-done
  82.5 0.6 copy.8
Async XLA Ops:
  77.9 4.6 %copy-start = (f32[8,8,256]{2,1,0:T(8,128)S(1)}, f32[8,8,256]{2,1,0:T(8,128)}, u32[]{:S(2)}) copy-start(f32[8,8,256]{2,1,0:T(8,128)} %get-tuple-element.5) | copy-start | bytes 196612

commit v2 on v1

v2 whole, which is shorter than its diff:
```python
import functools

import jax
import jax.numpy as jnp
from jax import lax
from jax.experimental import pallas as pl
from jax.experimental.pallas import tpu as pltpu
from jax.sharding import PartitionSpec as P

MESH = pl.DeviceIdType.MESH
F32 = jnp.float32
BF16 = jnp.bfloat16
OUT = pltpu.VMEM
VMEM_LIMIT = 48 * 1024 * 1024


def chunk_order(nz):
    half = nz // 2
    far = [half]
    for d in range(half - 1, 0, -1):
        far += [d, -d]
    return far + [0]


def chunk_blocks(nz):
    sizes = [1] + [2] * (nz // 2 - 2) + [3]
    starts = [sum(sizes[:i]) for i in range(len(sizes))]
    return [list(range(a, a + m)) for a, m in zip(starts, sizes)]


def kernel(
    nz, ny, trans, entry, share, cum_out, pooled,
    own, hp, hn, mon, pre, t0s, t0r, late, qs, qb, carry, outc, cab, wa, wb, ra, rb, rya, ryb,
    own_sem, fs_sem, bs_sem, hp_sem, hn_sem, t0_sem, cs_sem, cr_sem, cf_sem,
    as_sem, ar_sem, bzs_sem, bzr_sem, yas_sem, yar_sem, ybs_sem, ybr_sem,
):
    n = own.shape[-1]
    half = nz // 2
    rows = n // nz
    sub = rows // ny
    order = chunk_order(nz)
    tm = lax.axis_index("tm")
    co = lax.axis_index("cohort")
    ntm = lax.axis_size("tm")
    core, chip = lax.rem(tm, 2), tm // 2
    z, y = co // ny, lax.rem(co, ny)
    has_prev, has_next = tm > 0, tm < ntm - 1
    first_chip, last_chip = chip == 0, chip == ntm // 2 - 1
    z_up = lax.rem(z + 1, nz) * ny + y
    z_down = lax.rem(z + nz - 1, nz) * ny + y

    def y_peer(o):
        return lax.rem(y + o, ny)

    barrier = pltpu.get_barrier_semaphore()

    def greet(t, c):
        pl.semaphore_signal(barrier, inc=1, device_id=(t, c), device_id_type=MESH)

    near = (
        (has_prev, tm - 1), (has_next, tm + 1),
        ((core == 1) & (tm > 1), tm - 2), ((core == 1) & (tm < ntm - 2), tm + 2),
    )
    peers = 1 + ny
    for cond, t in near:
        pl.when(cond)(functools.partial(greet, t, co))
        peers = peers + jnp.where(cond, 1, 0)
    for c in [z_up, z_down] + [z * ny + y_peer(o) for o in range(1, ny)]:
        greet(tm, c)
    pl.semaphore_wait(barrier, peers)

    def remote(src, dst, ss, rs, t, c):
        return pltpu.make_async_remote_copy(
            src_ref=src, dst_ref=dst, send_sem=ss, recv_sem=rs, device_id=(t, c), device_id_type=MESH
        )

    def fwd_halo(i):
        return remote(trans.at[5 + i], hp.at[i], fs_sem.at[i], hp_sem.at[i], tm + 1, co)

    def bwd_halo(i):
        return remote(trans.at[i], hn.at[i], bs_sem.at[i], hn_sem.at[i], tm - 1, co)

    def own_copy(i):
        return pltpu.make_async_copy(trans.at[i], own.at[i], own_sem.at[i])

    @pl.when(has_next)
    def _():
        for i in (2, 1, 0):
            fwd_halo(i).start()

    @pl.when(has_prev)
    def _():
        for i in (0, 1, 2):
            bwd_halo(i).start()

    for i in range(8):
        own_copy(i).start()

    @pl.when(jnp.logical_not(has_prev))
    def _():
        hp[...] = jnp.zeros_like(hp)

    @pl.when(jnp.logical_not(has_next))
    def _():
        hn[...] = jnp.zeros_like(hn)

    strip = min(64, n)

    def graduate(t):
        def at(e):
            return (hp, e + 3) if e < 0 else ((hn, e - 8) if e > 7 else (own, e))

        edge = {0: 10, 1: 13, 2: 15, 5: 15, 6: 13, 7: 10}.get(t)
        scale = 1.0 / 16
        if edge is not None:
            scale = jnp.where(tm == (0 if t < 3 else ntm - 1), F32(1.0 / edge), F32(1.0 / 16))

        def step(i, _):
            g, r0 = i // (n // strip), pl.multiple_of(lax.rem(i, n // strip) * strip, strip)
            act = jnp.where(8 * tm + t >= entry[g], F32(1.0), F32(0.0))

            def load(e):
                ref, k = at(e)
                return ref[k, g, pl.ds(r0, strip), :]

            total = (
                4.0 * load(t) + 3.0 * (load(t - 1) + load(t + 1))
                + 2.0 * (load(t - 2) + load(t + 2)) + (load(t - 3) + load(t + 3))
            )
            row = lax.broadcasted_iota(jnp.int32, (strip, n), 0) + r0
            col = lax.broadcasted_iota(jnp.int32, (strip, n), 1)
            unit = jnp.where(row == col, 1.0 - act, 0.0)
            v = total * (act * scale) + unit
            hi = v.astype(BF16)
            mon[t, g, 0, pl.ds(r0, strip), :] = hi
            mon[t, g, 1, pl.ds(r0, strip), :] = (v - hi.astype(F32)).astype(BF16)
            return 0

        lax.fori_loop(0, 2 * (n // strip), step, 0)

    def dot(a, b):
        return jnp.dot(a, b, preferred_element_type=F32)

    def times(a, b):
        r = a.shape[1]
        both = dot(a.reshape(2 * r, n), b[0])
        return both[:r] + both[r:] + dot(a[0], b[1])

    def halves(ref, v):
        hi = v.astype(BF16)
        ref[0] = hi
        ref[1] = (v - hi.astype(F32)).astype(BF16)

    def multiply(dst, a, b, keep=None):
        def step(g, _):
            v = times(a(g), b(g))
            halves(dst.at[g], v)
            if keep is not None:
                keep[g] = v
            return 0
        lax.fori_loop(0, 2, step, 0)

    def take(ref, k):
        return lambda g: ref[k, g]

    def copy_pre(t):
        pre[t] = mon[t]

    def fwd_wait(i):
        pl.when(has_prev)(lambda: fwd_halo(i).wait_recv())

    def bwd_wait(i):
        pl.when(has_next)(lambda: bwd_halo(i).wait_recv())

    for i in range(8):
        own_copy(i).wait()
    graduate(3)
    graduate(4)

    def send_t0():
        return remote(t0s, t0r, t0_sem.at[0], t0_sem.at[1], tm + 1, co)

    @pl.when(core == 0)
    def _():
        for i in range(3):
            bwd_wait(i)
            graduate(5 + i)
        copy_pre(3)
        for t in range(4, 8):
            multiply(pre.at[t], take(pre, t - 1), take(mon, t))
        fwd_wait(2)
        graduate(2)
        fwd_wait(1)
        graduate(1)
        copy_pre(1)
        multiply(pre.at[2], take(mon, 1), take(mon, 2))
        for t in range(3, 8):
            multiply(pre.at[t], take(pre, 2), take(pre, t))
        row = lax.broadcasted_iota(jnp.int32, (n, n), 0)
        col = lax.broadcasted_iota(jnp.int32, (n, n), 1)
        for g in range(2):
            halves(pre.at[0, g], jnp.where(row == col, F32(1.0), F32(0.0)))
        fwd_wait(0)
        graduate(0)
        multiply(qb, take(mon, 0), take(pre, 7), t0s)
        send_t0().start()
        late[...] = mon[0]

    @pl.when(core == 1)
    def _():
        for i in (2, 1, 0):
            fwd_wait(i)
            graduate(i)
        copy_pre(0)
        for t in range(1, 5):
            multiply(pre.at[t], take(pre, t - 1), take(mon, t))
        for t in range(5, 8):
            bwd_wait(t - 5)
            graduate(t)
            multiply(pre.at[t], take(pre, t - 1), take(mon, t))
        send_t0().wait_recv()
        for g in range(2):
            halves(late.at[g], t0r[g])
        pl.when(jnp.logical_not(last_chip))(
            lambda: multiply(qb, lambda g: late[g], take(pre, 7), qs)
        )

    def chunk(j):
        return lax.rem(z + nz + order[j], nz)

    def chunk_rows(j):
        return pl.ds(pl.multiple_of(chunk(j) * rows, rows), rows)

    def carry_on(j, first):
        src = qs.at[:, chunk_rows(j), :] if first else outc.at[j]
        return remote(src, carry.at[j], cs_sem.at[j], cr_sem.at[j], tm + 2, co)

    def carry_back(j):
        return remote(carry.at[j], carry.at[j], cf_sem.at[j], cr_sem.at[j], tm - 1, co)

    @pl.when(first_chip)
    def _():
        row = lax.broadcasted_iota(jnp.int32, (rows, n), 0)
        col = lax.broadcasted_iota(jnp.int32, (rows, n), 1)
        pl.when(core == 1)(lambda: [carry_on(j, True).start() for j in range(nz)] and None)
        for j in range(nz):
            unit = jnp.where(row + chunk(j) * rows == col, F32(1.0), F32(0.0))
            for g in range(2):
                carry[j, g] = unit

    @pl.when(jnp.logical_not(first_chip) & jnp.logical_not(last_chip) & (core == 1))
    def _():
        for j in range(nz):
            carry_on(j, False).wait_recv()
            carry_back(j).start()
            for g in range(2):
                v = carry[j, g]
                hi = v.astype(BF16)
                outc[j, g] = times(jnp.stack([hi, (v - hi.astype(F32)).astype(BF16)]), qb[g])
            carry_on(j, False).start()

    sides = (z_up, z_down)

    def near(d, s):
        return order.index(half - s if d == 0 or s == 0 else s - half)

    def span(d, s):
        return (2 * d, 2) if s == 0 else (0, 4)

    def a_copy(d, s):
        m, c = span(d, s)
        src = wa.at[near(d, 0), pl.ds(m, c)] if s == 0 else ra.at[d, s - 1]
        return remote(src, ra.at[d, s, pl.ds(m, c)], as_sem.at[d, s], ar_sem.at[d, s], tm, sides[d])

    def a_step(d, s):
        j = near(d, s)
        if s > 0:
            a_copy(d, s - 1).wait_recv()
            m, c = span(d, s - 1)
            if c == 4:
                ra[d, s - 1] += wa[j]
            else:
                o = 2 - m
                ra[d, s - 1, m : m + 2] += wa[j, m : m + 2]
                ra[d, s - 1, o : o + 2] = wa[j, o : o + 2]
        a_copy(d, s).start()

    def yb_copy(j, o):
        src = wb.at[j, :, pl.ds(pl.multiple_of(y_peer(o) * sub, sub), sub), :]
        return remote(
            src, ryb.at[j, o - 1], ybs_sem.at[j, o - 1], ybr_sem.at[j, o - 1], tm, z * ny + y_peer(o)
        )

    summed = set()

    def yb_sum(j):
        if j not in summed:
            summed.add(j)
            for o in range(1, ny):
                yb_copy(j, o).wait_recv()
            v = wb[j, :, pl.ds(pl.multiple_of(y * sub, sub), sub), :]
            for o in range(1, ny):
                v = v + ryb[j, o - 1]
            rb[0, half + 1 + j] = v
        return rb[0, half + 1 + j]

    def b_copy(d, s):
        m, c = span(d, s)
        return remote(
            rb.at[d, s, pl.ds(m, c)], rb.at[d, s + 1, pl.ds(m, c)], bzs_sem.at[d, s], bzr_sem.at[d, s], tm, sides[d]
        )

    def b_step(d, s):
        v = yb_sum(near(d, s))
        if s > 0:
            b_copy(d, s - 1).wait_recv()
            m, c = span(d, s - 1)
            if c == 4:
                rb[d, s] += v
            else:
                o = 2 - m
                rb[d, s, m : m + 2] += v[m : m + 2]
                rb[d, s, o : o + 2] = v[o : o + 2]
        else:
            m, c = span(d, 0)
            rb[d, 0, m : m + c] = v[m : m + c]
        b_copy(d, s).start()

    blocks = chunk_blocks(nz)
    for k, block in enumerate(blocks):
        first, size = block[0], len(block)
        r = size * rows
        for j in block:
            @pl.when(jnp.logical_not(first_chip) & last_chip & (core == 1))
            def _():
                carry_on(j, False).wait_recv()
                carry_back(j).start()

            @pl.when(jnp.logical_not(first_chip) & (core == 0))
            def _():
                carry_back(j).wait_recv()

        def enter(g, _):
            v = carry[first : first + size, g].reshape(r, n)
            hi = v.astype(BF16)
            h = times(jnp.stack([hi, (v - hi.astype(F32)).astype(BF16)]), late[g])
            hi = h.astype(BF16)
            cab[g, 0, :r] = hi
            cab[g, 1, :r] = (h - hi.astype(F32)).astype(BF16)
            return 0

        lax.fori_loop(0, 2, enter, 0)

        def month(t, dst, m):
            total = None
            for g in range(2):
                v = times(cab[g, :, :r], pre[t, g])
                for i, j in enumerate(block):
                    cum_out[t, g, chunk_rows(j), :] = v[i * rows : (i + 1) * rows]
                w = share[g] * v
                total = w if total is None else total + w
            for i, j in enumerate(block):
                dst[j, m] = total[i * rows : (i + 1) * rows]

        def b_month(m, _):
            month(m + 4, wb, m)
            return 0

        def a_month(m, _):
            month(m, wa, m)
            return 0

        lax.fori_loop(0, 4, b_month, 0)
        for j in block:
            for o in range(1, ny):
                yb_copy(j, o).start()
        lax.fori_loop(0, 4, a_month, 0)
        for d in range(2):
            a_step(d, k)
        if k > 0:
            for d in range(2):
                b_step(d, k - 1)

    for s in range(len(blocks), half):
        for d in range(2):
            a_step(d, s)
        for d in range(2):
            b_step(d, s - 1)

    own_at = nz - 1
    v = wa[own_at]
    for d in range(2):
        a_copy(d, half - 1).wait_recv()
        v = v + ra[d, half - 1]
    wa[own_at] = v

    def ya_copy(o):
        src = wa.at[own_at, :, pl.ds(pl.multiple_of(y_peer(o) * sub, sub), sub), :]
        return remote(src, rya.at[o - 1], yas_sem.at[o - 1], yar_sem.at[o - 1], tm, z * ny + y_peer(o))

    for o in range(1, ny):
        ya_copy(o).start()
    for d in range(2):
        b_step(d, half - 1)
    v = yb_sum(own_at)
    for d in range(2):
        b_copy(d, half - 1).wait_recv()
        v = v + rb[d, half]
    pooled[4:8] = v
    v = wa[own_at, :, pl.ds(pl.multiple_of(y * sub, sub), sub), :]
    for o in range(1, ny):
        ya_copy(o).wait_recv()
        v = v + rya[o - 1]
    pooled[0:4] = v

    for i in range(3):
        pl.when(has_next)(lambda: fwd_halo(i).wait_send())
        pl.when(has_prev)(lambda: bwd_halo(i).wait_send())
    pl.when(core == 0)(lambda: send_t0().wait_send())
    for j in range(nz):
        pl.when((core == 1) & jnp.logical_not(last_chip))(lambda: carry_on(j, False).wait_send())
        pl.when((core == 1) & jnp.logical_not(first_chip))(lambda: carry_back(j).wait_send())
        for o in range(1, ny):
            yb_copy(j, o).wait_send()
    for d in range(2):
        for s in range(half):
            a_copy(d, s).wait_send()
            b_copy(d, s).wait_send()
    for o in range(1, ny):
        ya_copy(o).wait_send()


def on_device(nz, ny, transition, entry, share):
    n = transition.shape[-1]
    half, rows = nz // 2, n // nz
    sub = rows // ny
    widest = max(len(b) for b in chunk_blocks(nz))
    dma = pltpu.SemaphoreType.DMA
    return pl.pallas_call(
        functools.partial(kernel, nz, ny),
        out_shape=(
            OUT(transition.shape, F32),
            OUT((8, sub, n), F32),
        ),
        in_specs=[
            pl.BlockSpec(memory_space=pl.ANY),
            pl.BlockSpec(memory_space=pltpu.SMEM),
            pl.BlockSpec(memory_space=pltpu.SMEM),
        ],
        out_specs=(pl.BlockSpec(memory_space=pltpu.VMEM), pl.BlockSpec(memory_space=pltpu.VMEM)),
        scratch_shapes=[
            pltpu.VMEM((8, 2, n, n), F32),
            pltpu.VMEM((3, 2, n, n), F32),
            pltpu.VMEM((3, 2, n, n), F32),
            pltpu.VMEM((8, 2, 2, n, n), BF16),
            pltpu.VMEM((8, 2, 2, n, n), BF16),
            pltpu.VMEM((2, n, n), F32),
            pltpu.VMEM((2, n, n), F32),
            pltpu.VMEM((2, 2, n, n), BF16),
            pltpu.VMEM((2, n, n), F32),
            pltpu.VMEM((2, 2, n, n), BF16),
            pltpu.VMEM((nz, 2, rows, n), F32),
            pltpu.VMEM((nz, 2, rows, n), F32),
            pltpu.VMEM((2, 2, widest * rows, n), BF16),
            pltpu.VMEM((nz, 4, rows, n), F32),
            pltpu.VMEM((nz, 4, rows, n), F32),
            pltpu.VMEM((2, half, 4, rows, n), F32),
            pltpu.VMEM((2, half + 1 + nz, 4, sub, n), F32),
            pltpu.VMEM((ny - 1, 4, sub, n), F32),
            pltpu.VMEM((nz, ny - 1, 4, sub, n), F32),
            dma((8,)), dma((3,)), dma((3,)), dma((3,)), dma((3,)), dma((2,)),
            dma((nz,)), dma((nz,)), dma((nz,)),
            dma((2, half)), dma((2, half)), dma((2, half)), dma((2, half)),
            dma((ny - 1,)), dma((ny - 1,)), dma((nz, ny - 1)), dma((nz, ny - 1)),
        ],
        compiler_params=pltpu.CompilerParams(
            collective_id=0, has_side_effects=True, vmem_limit_bytes=VMEM_LIMIT
        ),
        cost_estimate=pl.CostEstimate(
            flops=3 * 2 * 46 * n**3, bytes_accessed=2 * 4 * 16 * n * n, transcendentals=0
        ),
    )(transition, entry, share)


def solution(mesh, nz=8, ny=4):
    return jax.shard_map(
        functools.partial(on_device, nz, ny),
        mesh=mesh,
        in_specs=(P("tm", "cohort", None, None), P("cohort"), P("cohort")),
        out_specs=(P("tm", "cohort", None, None), P("tm", "cohort", None)),
        check_vma=False,
    )
```

time: 83.3 us -> 66.7 us (0.80)
  Pallas kernels: 77.3 us -> 61.2 us
  local copies, waits for them, and re-layouts: 5.26 us -> 3.95 us
    pallas_call x1, Pallas kernels: 77.3 us -> 61.2 us  [on_device(): pl.pallas_call(functools.partial(kernel, nz, ny), out_shape=(OUT(transiti...]
    unnamed x4 -> x6, local copies, waits for them, and re-layouts: 5.26 us -> 3.95 us
where the time goes in v2:
time: 66.7 us; the launch traced here: 65.8 us
  Pallas kernels  61.2 us (92%)
  local copies, waits for them, and re-layouts  3.95 us (6%)
    pallas_call x1, Pallas kernels, on_device(): pl.pallas_call(functools.partial(kernel, nz, ny), out_shape=(OUT(transiti...  61.2 us
    unnamed x6, local copies, waits for them, and re-layouts  3.95 us

profile of v2, /device:TPU:6, one launch (start us, length us, event | category | flops | bytes accessed | tf_op | source)
XLA Modules:
  0.0 65.8 jit_solution(2565589271255759380)
XLA Ops:
  0.6 0.0 copy-start
  0.6 0.6 copy-done
  1.3 0.0 copy-start.1
  1.3 0.7 copy-done.1
  1.9 61.2 %shard_map.50 = (f32[8,2,256,256]{3,2,1,0:T(8,128)S(1)}, f32[8,8,256]{2,1,0:T(8,128)S(1)}) custom-call(f32[8,2,256,256]{3,2,1,0:T(8,128)} %trans.1, s32[2]{0:T(128)S(1)} %copy-done, f32[2]{0:T(128)S(1)} %copy-done.1), custom_call_target="tpu_custom_call" | custom-call | flops 4630511616 | bytes 8388608 | tf_op jit(solution)/shard_map/pallas_call | solution.py:439
  63.2 2.0 %copy.7 = f32[8,2,256,256]{3,2,1,0:T(8,128)} copy(f32[8,2,256,256]{3,2,1,0:T(8,128)S(1)} %get-tuple-element.2) | data formatting | bytes 8388608
  65.2 0.6 copy.8
Async XLA Ops:
  0.6 0.7 copy-start
  1.3 0.7 copy-start.1

commit v3 on v2

--- a/solution.py
+++ b/solution.py
@@ -14,31 +14,26 @@
 VMEM_LIMIT = 48 * 1024 * 1024
 
 
-def chunk_order(nz):
+def chunk_blocks(nz):
     half = nz // 2
-    far = [half]
-    for d in range(half - 1, 0, -1):
-        far += [d, -d]
-    return far + [0]
-
-
-def chunk_blocks(nz):
-    sizes = [1] + [2] * (nz // 2 - 2) + [3]
-    starts = [sum(sizes[:i]) for i in range(len(sizes))]
-    return [list(range(a, a + m)) for a, m in zip(starts, sizes)]
+    blocks = [[d, -d] for d in range(half - 1, 0, -1)]
+    blocks[0].insert(0, half)
+    blocks[-1].append(0)
+    return blocks
 
 
 def kernel(
-    nz, ny, trans, entry, share, cum_out, pooled,
-    own, hp, hn, mon, pre, t0s, t0r, late, qs, qb, carry, outc, cab, wa, wb, ra, rb, rya, ryb,
-    own_sem, fs_sem, bs_sem, hp_sem, hn_sem, t0_sem, cs_sem, cr_sem, cf_sem,
-    as_sem, ar_sem, bzs_sem, bzr_sem, yas_sem, yar_sem, ybs_sem, ybr_sem,
+    nz, ny, trans, entry_in, share_in, cum_out, pooled, entry, share,
+    own, hp, hn, mon, pre, t0s, t0r, late, qs, qb, carry, outc, cab, wa, wb, ra, fa, rb, fb, rya, ryb, ysum,
+    in_sem, own_sem, fs_sem, bs_sem, hp_sem, hn_sem, t0_sem, cs_sem, cr_sem, cf_sem,
+    as_sem, ar_sem, fas_sem, far_sem, bzs_sem, bzr_sem, fbs_sem, fbr_sem, yas_sem, yar_sem, ybs_sem, ybr_sem,
 ):
     n = own.shape[-1]
     half = nz // 2
     rows = n // nz
     sub = rows // ny
-    order = chunk_order(nz)
+    blocks = chunk_blocks(nz)
+    order = sum(blocks, [])
     tm = lax.axis_index("tm")
     co = lax.axis_index("cohort")
     ntm = lax.axis_size("tm")
@@ -46,11 +41,16 @@
     z, y = co // ny, lax.rem(co, ny)
     has_prev, has_next = tm > 0, tm < ntm - 1
     first_chip, last_chip = chip == 0, chip == ntm // 2 - 1
-    z_up = lax.rem(z + 1, nz) * ny + y
-    z_down = lax.rem(z + nz - 1, nz) * ny + y
+
+    def z_at(k):
+        return lax.rem(z + nz + k, nz) * ny + y
 
     def y_peer(o):
         return lax.rem(y + o, ny)
+
+    small = [pltpu.make_async_copy(entry_in, entry, in_sem.at[0]), pltpu.make_async_copy(share_in, share, in_sem.at[1])]
+    for copy in small:
+        copy.start()
 
     barrier = pltpu.get_barrier_semaphore()
 
@@ -61,11 +61,11 @@
         (has_prev, tm - 1), (has_next, tm + 1),
         ((core == 1) & (tm > 1), tm - 2), ((core == 1) & (tm < ntm - 2), tm + 2),
     )
-    peers = 1 + ny
+    peers = 3 + ny
     for cond, t in near:
         pl.when(cond)(functools.partial(greet, t, co))
         peers = peers + jnp.where(cond, 1, 0)
-    for c in [z_up, z_down] + [z * ny + y_peer(o) for o in range(1, ny)]:
+    for c in [z_at(k) for k in (1, -1, 2, -2)] + [z * ny + y_peer(o) for o in range(1, ny)]:
         greet(tm, c)
     pl.semaphore_wait(barrier, peers)
 
@@ -83,15 +83,17 @@
     def own_copy(i):
         return pltpu.make_async_copy(trans.at[i], own.at[i], own_sem.at[i])
 
-    @pl.when(has_next)
-    def _():
+    def send_fwd():
         for i in (2, 1, 0):
             fwd_halo(i).start()
 
-    @pl.when(has_prev)
-    def _():
+    def send_bwd():
         for i in (0, 1, 2):
             bwd_halo(i).start()
+
+    pl.when((core == 0) & has_prev)(send_bwd)
+    pl.when(has_next)(send_fwd)
+    pl.when((core == 1) & has_prev)(send_bwd)
 
     for i in range(8):
         own_copy(i).start()
@@ -172,6 +174,8 @@
     def bwd_wait(i):
         pl.when(has_next)(lambda: bwd_halo(i).wait_recv())
 
+    for copy in small:
+        copy.wait()
     for i in range(8):
         own_copy(i).wait()
     graduate(3)
@@ -231,64 +235,73 @@
     def chunk_rows(j):
         return pl.ds(pl.multiple_of(chunk(j) * rows, rows), rows)
 
-    def carry_on(j, first):
-        src = qs.at[:, chunk_rows(j), :] if first else outc.at[j]
-        return remote(src, carry.at[j], cs_sem.at[j], cr_sem.at[j], tm + 2, co)
-
-    def carry_back(j):
-        return remote(carry.at[j], carry.at[j], cf_sem.at[j], cr_sem.at[j], tm - 1, co)
+    def carry_on(j, g, first=False):
+        src = qs.at[g, chunk_rows(j), :] if first else outc.at[j, g]
+        return remote(src, carry.at[j, g], cs_sem.at[j, g], cr_sem.at[j, g], tm + 2, co)
+
+    def carry_back(j, g):
+        return remote(carry.at[j, g], carry.at[j, g], cf_sem.at[j, g], cr_sem.at[j, g], tm - 1, co)
+
+    pieces = [(j, g) for j in range(nz) for g in range(2)]
 
     @pl.when(first_chip)
     def _():
         row = lax.broadcasted_iota(jnp.int32, (rows, n), 0)
         col = lax.broadcasted_iota(jnp.int32, (rows, n), 1)
-        pl.when(core == 1)(lambda: [carry_on(j, True).start() for j in range(nz)] and None)
+        pl.when(core == 1)(lambda: [carry_on(j, g, True).start() for j, g in pieces] and None)
         for j in range(nz):
             unit = jnp.where(row + chunk(j) * rows == col, F32(1.0), F32(0.0))
             for g in range(2):
                 carry[j, g] = unit
 
-    @pl.when(jnp.logical_not(first_chip) & jnp.logical_not(last_chip) & (core == 1))
-    def _():
-        for j in range(nz):
-            carry_on(j, False).wait_recv()
-            carry_back(j).start()
-            for g in range(2):
-                v = carry[j, g]
-                hi = v.astype(BF16)
-                outc[j, g] = times(jnp.stack([hi, (v - hi.astype(F32)).astype(BF16)]), qb[g])
-            carry_on(j, False).start()
-
-    sides = (z_up, z_down)
-
-    def near(d, s):
-        return order.index(half - s if d == 0 or s == 0 else s - half)
-
-    def span(d, s):
-        return (2 * d, 2) if s == 0 else (0, 4)
-
-    def a_copy(d, s):
-        m, c = span(d, s)
-        src = wa.at[near(d, 0), pl.ds(m, c)] if s == 0 else ra.at[d, s - 1]
-        return remote(src, ra.at[d, s, pl.ds(m, c)], as_sem.at[d, s], ar_sem.at[d, s], tm, sides[d])
-
-    def a_step(d, s):
-        j = near(d, s)
-        if s > 0:
-            a_copy(d, s - 1).wait_recv()
-            m, c = span(d, s - 1)
-            if c == 4:
-                ra[d, s - 1] += wa[j]
-            else:
-                o = 2 - m
-                ra[d, s - 1, m : m + 2] += wa[j, m : m + 2]
-                ra[d, s - 1, o : o + 2] = wa[j, o : o + 2]
-        a_copy(d, s).start()
-
-    def yb_copy(j, o):
-        src = wb.at[j, :, pl.ds(pl.multiple_of(y_peer(o) * sub, sub), sub), :]
+    middle = jnp.logical_not(first_chip) & jnp.logical_not(last_chip) & (core == 1)
+
+    def hand_on(some):
+        for j, g in some:
+            carry_on(j, g).wait_recv()
+            v = carry[j, g]
+            hi = v.astype(BF16)
+            outc[j, g] = times(jnp.stack([hi, (v - hi.astype(F32)).astype(BF16)]), qb[g])
+            carry_on(j, g).start()
+            carry_back(j, g).start()
+
+    ahead = min(2 * nz, 2 * len(blocks[0]) + 4)
+    pl.when(middle)(lambda: hand_on(pieces[:ahead]))
+
+    def place(d, s):
+        return order.index(half - s if d == 0 else s - half)
+
+    def z_side(d, k=1):
+        return z_at(k if d == 0 else -k)
+
+    def a_copy(d, s, m):
+        src = wa.at[place(d, 1), m] if s == 1 else ra.at[d, s - 2, m]
+        return remote(src, ra.at[d, s - 1, m], as_sem.at[d, s - 1, m], ar_sem.at[d, s - 1, m], tm, z_side(d))
+
+    def a_far(d, i):
+        return remote(wa.at[0, 2 * d + i], fa.at[d, i], fas_sem.at[d, i], far_sem.at[d, i], tm, z_side(d, 2))
+
+    def a_come(d, s, m):
+        parts = []
+        if s >= 2:
+            a_copy(d, s - 1, m).wait_recv()
+            parts.append(ra[d, s - 2, m])
+        if s == 2 and m // 2 == d:
+            a_far(d, m % 2).wait_recv()
+            parts.append(fa[d, m % 2])
+        return parts
+
+    def a_stage(s, months=range(4)):
+        for m in months:
+            for d in range(2):
+                ra[d, s - 2, m] = sum(a_come(d, s, m), wa[place(d, s), m])
+                a_copy(d, s, m).start()
+
+    def yb_copy(j, h, o):
+        rows_to = pl.ds(pl.multiple_of(y_peer(o) * sub, sub), sub)
         return remote(
-            src, ryb.at[j, o - 1], ybs_sem.at[j, o - 1], ybr_sem.at[j, o - 1], tm, z * ny + y_peer(o)
+            wb.at[j, pl.ds(2 * h, 2), rows_to, :], ryb.at[j, o - 1, pl.ds(2 * h, 2)],
+            ybs_sem.at[j, h, o - 1], ybr_sem.at[j, h, o - 1], tm, z * ny + y_peer(o),
         )
 
     summed = set()
@@ -296,49 +309,55 @@
     def yb_sum(j):
         if j not in summed:
             summed.add(j)
-            for o in range(1, ny):
-                yb_copy(j, o).wait_recv()
             v = wb[j, :, pl.ds(pl.multiple_of(y * sub, sub), sub), :]
             for o in range(1, ny):
+                for h in range(2):
+                    yb_copy(j, h, o).wait_recv()
                 v = v + ryb[j, o - 1]
-            rb[0, half + 1 + j] = v
-        return rb[0, half + 1 + j]
+            ysum[j] = v
 
     def b_copy(d, s):
-        m, c = span(d, s)
+        return remote(rb.at[d, s - 1], rb.at[d, s], bzs_sem.at[d, s - 1], bzr_sem.at[d, s - 1], tm, z_side(d))
+
+    def b_far(d):
         return remote(
-            rb.at[d, s, pl.ds(m, c)], rb.at[d, s + 1, pl.ds(m, c)], bzs_sem.at[d, s], bzr_sem.at[d, s], tm, sides[d]
+            ysum.at[0, pl.ds(2 * d, 2)], fb.at[d], fbs_sem.at[d], fbr_sem.at[d], tm, z_side(d, 2)
         )
 
-    def b_step(d, s):
-        v = yb_sum(near(d, s))
-        if s > 0:
-            b_copy(d, s - 1).wait_recv()
-            m, c = span(d, s - 1)
-            if c == 4:
-                rb[d, s] += v
+    def b_stage(s):
+        if s == 1:
+            yb_sum(0)
+            for d in range(2):
+                b_far(d).start()
+        for d in range(2):
+            j = place(d, s)
+            yb_sum(j)
+            if s == 1:
+                rb[d, 0] = ysum[j]
             else:
-                o = 2 - m
-                rb[d, s, m : m + 2] += v[m : m + 2]
-                rb[d, s, o : o + 2] = v[o : o + 2]
-        else:
-            m, c = span(d, 0)
-            rb[d, 0, m : m + c] = v[m : m + c]
-        b_copy(d, s).start()
-
-    blocks = chunk_blocks(nz)
-    for k, block in enumerate(blocks):
-        first, size = block[0], len(block)
+                b_copy(d, s - 1).wait_recv()
+                rb[d, s - 1] += ysum[j]
+            if s == 2:
+                b_far(d).wait_recv()
+                rb[d, 1, 2 * d : 2 * d + 2] += fb[d]
+            b_copy(d, s).start()
+
+    first = 0
+    for k in range(len(blocks)):
+        size = len(blocks[k])
+        block = range(first, first + size)
         r = size * rows
         for j in block:
             @pl.when(jnp.logical_not(first_chip) & last_chip & (core == 1))
             def _():
-                carry_on(j, False).wait_recv()
-                carry_back(j).start()
+                for g in range(2):
+                    carry_on(j, g).wait_recv()
+                    carry_back(j, g).start()
 
             @pl.when(jnp.logical_not(first_chip) & (core == 0))
             def _():
-                carry_back(j).wait_recv()
+                for g in range(2):
+                    carry_back(j, g).wait_recv()
 
         def enter(g, _):
             v = carry[first : first + size, g].reshape(r, n)
@@ -370,29 +389,36 @@
             month(m, wa, m)
             return 0
 
-        lax.fori_loop(0, 4, b_month, 0)
-        for j in block:
-            for o in range(1, ny):
-                yb_copy(j, o).start()
-        lax.fori_loop(0, 4, a_month, 0)
+        for h in range(2):
+            if k == 0:
+                for m in (2 * h, 2 * h + 1):
+                    month(m, wa, m)
+                    for d in range(2):
+                        a_copy(d, 1, m).start()
+                    a_far(h, m % 2).start()
+            else:
+                lax.fori_loop(2 * h, 2 * h + 2, a_month, 0)
+            lax.fori_loop(2 * h, 2 * h + 2, b_month, 0)
+            for j in block:
+                for o in range(1, ny):
+                    yb_copy(j, h, o).start()
+            if k == len(blocks) - 1 and half > 2:
+                a_stage(2, (2 * h, 2 * h + 1))
+        if k == 0 and ahead < 2 * nz:
+            pl.when(middle)(lambda: hand_on(pieces[ahead:]))
+        first += size
+
+    for s in range(1, half - 1):
+        if s > 1:
+            a_stage(s + 1)
+        b_stage(s)
+
+    own_at = nz - 1
+    for m in range(4):
+        v = wa[own_at, m]
         for d in range(2):
-            a_step(d, k)
-        if k > 0:
-            for d in range(2):
-                b_step(d, k - 1)
-
-    for s in range(len(blocks), half):
-        for d in range(2):
-            a_step(d, s)
-        for d in range(2):
-            b_step(d, s - 1)
-
-    own_at = nz - 1
-    v = wa[own_at]
-    for d in range(2):
-        a_copy(d, half - 1).wait_recv()
-        v = v + ra[d, half - 1]
-    wa[own_at] = v
+            v = sum(a_come(d, half, m), v)
+        wa[own_at, m] = v
 
     def ya_copy(o):
         src = wa.at[own_at, :, pl.ds(pl.multiple_of(y_peer(o) * sub, sub), sub), :]
@@ -400,34 +426,55 @@
 
     for o in range(1, ny):
         ya_copy(o).start()
+    b_stage(half - 1)
+    for i in range(3):
+        pl.when(has_next)(lambda: fwd_halo(i).wait_send())
+        pl.when(has_prev)(lambda: bwd_halo(i).wait_send())
+    pl.when(core == 0)(lambda: send_t0().wait_send())
+    for j in range(nz):
+        for g in range(2):
+            pl.when((core == 1) & jnp.logical_not(last_chip))(lambda: carry_on(j, g).wait_send())
+            pl.when((core == 1) & jnp.logical_not(first_chip))(lambda: carry_back(j, g).wait_send())
+        for o in range(1, ny):
+            for h in range(2):
+                yb_copy(j, h, o).wait_send()
     for d in range(2):
-        b_step(d, half - 1)
-    v = yb_sum(own_at)
+        b_far(d).wait_send()
+        for i in range(2):
+            a_far(d, i).wait_send()
+        for s in range(1, half):
+            b_copy(d, s).wait_send()
+            for m in range(4):
+                a_copy(d, s, m).wait_send()
+
+    yb_sum(own_at)
+    v = ysum[own_at]
     for d in range(2):
         b_copy(d, half - 1).wait_recv()
-        v = v + rb[d, half]
+        v = v + rb[d, half - 1]
     pooled[4:8] = v
+    if half == 2:
+        for d in range(2):
+            b_far(d).wait_recv()
+            pooled[4 + 2 * d : 6 + 2 * d] += fb[d]
     v = wa[own_at, :, pl.ds(pl.multiple_of(y * sub, sub), sub), :]
     for o in range(1, ny):
         ya_copy(o).wait_recv()
         v = v + rya[o - 1]
     pooled[0:4] = v
-
-    for i in range(3):
-        pl.when(has_next)(lambda: fwd_halo(i).wait_send())
-        pl.when(has_prev)(lambda: bwd_halo(i).wait_send())
-    pl.when(core == 0)(lambda: send_t0().wait_send())
-    for j in range(nz):
-        pl.when((core == 1) & jnp.logical_not(last_chip))(lambda: carry_on(j, False).wait_send())
-        pl.when((core == 1) & jnp.logical_not(first_chip))(lambda: carry_back(j).wait_send())
-        for o in range(1, ny):
-            yb_copy(j, o).wait_send()
-    for d in range(2):
-        for s in range(half):
-            a_copy(d, s).wait_send()
-            b_copy(d, s).wait_send()
     for o in range(1, ny):
         ya_copy(o).wait_send()
+
+
+def deliver(cum, pooled, cum_out, pooled_out, sem):
+    copies = [pltpu.make_async_copy(pooled, pooled_out, sem.at[8])]
+    for i in range(8):
+        part = pl.ds(i, 1)
+        copies.append(pltpu.make_async_copy(cum.at[part], cum_out.at[part], sem.at[i]))
+    for copy in copies:
+        copy.start()
+    for copy in copies:
+        copy.wait()
 
 
 def on_device(nz, ny, transition, entry, share):
@@ -436,19 +483,21 @@
     sub = rows // ny
     widest = max(len(b) for b in chunk_blocks(nz))
     dma = pltpu.SemaphoreType.DMA
-    return pl.pallas_call(
+    cum, pooled = pl.pallas_call(
         functools.partial(kernel, nz, ny),
         out_shape=(
             OUT(transition.shape, F32),
             OUT((8, sub, n), F32),
         ),
         in_specs=[
-            pl.BlockSpec(memory_space=pl.ANY),
-            pl.BlockSpec(memory_space=pltpu.SMEM),
-            pl.BlockSpec(memory_space=pltpu.SMEM),
+            pl.BlockSpec(memory_space=pltpu.HBM),
+            pl.BlockSpec(memory_space=pltpu.HBM),
+            pl.BlockSpec(memory_space=pltpu.HBM),
         ],
         out_specs=(pl.BlockSpec(memory_space=pltpu.VMEM), pl.BlockSpec(memory_space=pltpu.VMEM)),
         scratch_shapes=[
+            pltpu.SMEM(entry.shape, entry.dtype),
+            pltpu.SMEM(share.shape, F32),
             pltpu.VMEM((8, 2, n, n), F32),
             pltpu.VMEM((3, 2, n, n), F32),
             pltpu.VMEM((3, 2, n, n), F32),
@@ -464,14 +513,18 @@
             pltpu.VMEM((2, 2, widest * rows, n), BF16),
             pltpu.VMEM((nz, 4, rows, n), F32),
             pltpu.VMEM((nz, 4, rows, n), F32),
-            pltpu.VMEM((2, half, 4, rows, n), F32),
-            pltpu.VMEM((2, half + 1 + nz, 4, sub, n), F32),
+            pltpu.VMEM((2, half - 1, 4, rows, n), F32),
+            pltpu.VMEM((2, 2, rows, n), F32),
+            pltpu.VMEM((2, half, 4, sub, n), F32),
+            pltpu.VMEM((2, 2, sub, n), F32),
             pltpu.VMEM((ny - 1, 4, sub, n), F32),
             pltpu.VMEM((nz, ny - 1, 4, sub, n), F32),
-            dma((8,)), dma((3,)), dma((3,)), dma((3,)), dma((3,)), dma((2,)),
-            dma((nz,)), dma((nz,)), dma((nz,)),
-            dma((2, half)), dma((2, half)), dma((2, half)), dma((2, half)),
-            dma((ny - 1,)), dma((ny - 1,)), dma((nz, ny - 1)), dma((nz, ny - 1)),
+            pltpu.VMEM((nz, 4, sub, n), F32),
+            dma((2,)), dma((8,)), dma((3,)), dma((3,)), dma((3,)), dma((3,)), dma((2,)),
+            dma((nz, 2)), dma((nz, 2)), dma((nz, 2)),
+            dma((2, half - 1, 4)), dma((2, half - 1, 4)), dma((2, 2)), dma((2, 2)),
+            dma((2, half - 1)), dma((2, half - 1)), dma((2,)), dma((2,)),
+            dma((ny - 1,)), dma((ny - 1,)), dma((nz, 2, ny - 1)), dma((nz, 2, ny - 1)),
         ],
         compiler_params=pltpu.CompilerParams(
             collective_id=0, has_side_effects=True, vmem_limit_bytes=VMEM_LIMIT
@@ -479,7 +532,15 @@
         cost_estimate=pl.CostEstimate(
             flops=3 * 2 * 46 * n**3, bytes_accessed=2 * 4 * 16 * n * n, transcendentals=0
         ),
-    )(transition, entry, share)
+    )(transition, *(pltpu.with_memory_space_constraint(a, pltpu.HBM) for a in (entry, share)))
+    return pl.pallas_call(
+        deliver,
+        out_shape=(jax.ShapeDtypeStruct(cum.shape, F32), jax.ShapeDtypeStruct(pooled.shape, F32)),
+        in_specs=[pl.BlockSpec(memory_space=pltpu.VMEM)] * 2,
+        out_specs=[pl.BlockSpec(memory_space=pl.ANY)] * 2,
+        scratch_shapes=[dma((9,))],
+        compiler_params=pltpu.CompilerParams(vmem_limit_bytes=1024 * 1024),
+    )(*(pltpu.with_memory_space_constraint(a, pltpu.VMEM) for a in (cum, pooled)))
 
 
 def solution(mesh, nz=8, ny=4):

time: 66.7 us -> 63.5 us (0.952); the launches traced: 65.8 us -> 63.4 us
  local copies, waits for them, and re-layouts: 3.95 us -> 0 us
  Pallas kernels: 61.2 us -> 62.8 us
    unnamed x6 -> x0, local copies, waits for them, and re-layouts: 3.95 us -> none
    pallas_call x0 -> x1, Pallas kernels: none -> 2.1 us  [on_device(): pl.pallas_call(deliver, out_shape=(jax.ShapeDtypeStruct(cum.shape, F32),...]
where the time goes in v3:
time: 63.5 us; the launch traced here: 63.4 us
  Pallas kernels  62.8 us (99%)
  between operations  0.64 us (1%)
    pallas_call x1, Pallas kernels, on_device(): pl.pallas_call(functools.partial(kernel, nz, ny), out_shape=(OUT(transiti...  60.7 us
    pallas_call x1, Pallas kernels, on_device(): pl.pallas_call(deliver, out_shape=(jax.ShapeDtypeStruct(cum.shape, F32),...  2.1 us

profile of v3, /device:TPU:6, one launch (start us, length us, event | category | flops | bytes accessed | tf_op | source)
XLA Modules:
  0.0 63.4 jit_solution(10452002566463777455)
XLA Ops:
  0.6 60.7 %shard_map.50 = (f32[8,2,256,256]{3,2,1,0:T(8,128)S(1)}, f32[8,8,256]{2,1,0:T(8,128)S(1)}) custom-call(f32[8,2,256,256]{3,2,1,0:T(8,128)} %trans.1, s32[2]{0:T(128)} %entry_in.1, f32[2]{0:T(128)} %share_in.1), custom_call_target="tpu_custom_call" | custom-call | flops 4630511616 | bytes 8388608 | tf_op jit(solution)/shard_map/pallas_call | solution.py:486
  61.3 2.1 %shard_map.51 = (f32[8,2,256,256]{3,2,1,0:T(8,128)}, f32[8,8,256]{2,1,0:T(8,128)}) custom-call(f32[8,2,256,256]{3,2,1,0:T(8,128)S(1)} %get-tuple-element.4.cum, f32[8,8,256]{2,1,0:T(8,128)S(1)} %get-tuple-element.5.pooled), custom_call_target="tpu_custom_call" | custom-call | tf_op jit(solution)/shard_map/pallas_call | solution.py:536

commit v4 on v3

--- a/solution.py
+++ b/solution.py
@@ -108,7 +108,7 @@
 
     strip = min(64, n)
 
-    def graduate(t):
+    def graduate(t, part=None, groups=None):
         def at(e):
             return (hp, e + 3) if e < 0 else ((hn, e - 8) if e > 7 else (own, e))
 
@@ -116,29 +116,40 @@
         scale = 1.0 / 16
         if edge is not None:
             scale = jnp.where(tm == (0 if t < 3 else ntm - 1), F32(1.0 / edge), F32(1.0 / 16))
+        last, other = (t - 3, t + 3) if t == 0 else (t + 3, t - 3)
+        strips = n // strip
+        low = 0 if groups is None else groups[0] * strips
+        high = 2 * strips if groups is None else (groups[-1] + 1) * strips
 
         def step(i, _):
-            g, r0 = i // (n // strip), pl.multiple_of(lax.rem(i, n // strip) * strip, strip)
-            act = jnp.where(8 * tm + t >= entry[g], F32(1.0), F32(0.0))
+            g, r0 = i // strips, pl.multiple_of(lax.rem(i, strips) * strip, strip)
+            here = pl.ds(r0, strip)
 
             def load(e):
                 ref, k = at(e)
-                return ref[k, g, pl.ds(r0, strip), :]
-
-            total = (
-                4.0 * load(t) + 3.0 * (load(t - 1) + load(t + 1))
-                + 2.0 * (load(t - 2) + load(t + 2)) + (load(t - 3) + load(t + 3))
-            )
+                return ref[k, g, here, :]
+
+            if groups is None:
+                total = (
+                    4.0 * load(t) + 3.0 * (load(t - 1) + load(t + 1))
+                    + 2.0 * (load(t - 2) + load(t + 2)) + load(other)
+                )
+                if part is not None:
+                    part[g, here, :] = total
+                    return 0
+            else:
+                total = part[g, here, :]
+            act = jnp.where(8 * tm + t >= entry[g], F32(1.0), F32(0.0))
             row = lax.broadcasted_iota(jnp.int32, (strip, n), 0) + r0
             col = lax.broadcasted_iota(jnp.int32, (strip, n), 1)
             unit = jnp.where(row == col, 1.0 - act, 0.0)
-            v = total * (act * scale) + unit
+            v = (total + load(last)) * (act * scale) + unit
             hi = v.astype(BF16)
-            mon[t, g, 0, pl.ds(r0, strip), :] = hi
-            mon[t, g, 1, pl.ds(r0, strip), :] = (v - hi.astype(F32)).astype(BF16)
+            mon[t, g, 0, here, :] = hi
+            mon[t, g, 1, here, :] = (v - hi.astype(F32)).astype(BF16)
             return 0
 
-        lax.fori_loop(0, 2 * (n // strip), step, 0)
+        lax.fori_loop(low, high, step, 0)
 
     def dot(a, b):
         return jnp.dot(a, b, preferred_element_type=F32)
@@ -181,8 +192,28 @@
     graduate(3)
     graduate(4)
 
-    def send_t0():
-        return remote(t0s, t0r, t0_sem.at[0], t0_sem.at[1], tm + 1, co)
+    def send_t0(g):
+        return remote(t0s.at[g], t0r.at[g], t0_sem.at[0, g], t0_sem.at[1, g], tm + 1, co)
+
+    def chunk(j):
+        return lax.rem(z + nz + order[j], nz)
+
+    def chunk_rows(j):
+        return pl.ds(pl.multiple_of(chunk(j) * rows, rows), rows)
+
+    def carry_on(j, g, first=False):
+        src = qs.at[g, chunk_rows(j), :] if first else outc.at[j, g]
+        return remote(src, carry.at[j, g], cs_sem.at[j, g], cr_sem.at[j, g], tm + 2, co)
+
+    def carry_back(j, g):
+        return remote(carry.at[j, g], carry.at[j, g], cf_sem.at[j, g], cr_sem.at[j, g], tm - 1, co)
+
+    pieces = [(j, g) for j in range(nz) for g in range(2)]
+
+    soon = len(blocks[0])
+
+    def take_late(g):
+        return late[g]
 
     @pl.when(core == 0)
     def _():
@@ -204,10 +235,12 @@
         col = lax.broadcasted_iota(jnp.int32, (n, n), 1)
         for g in range(2):
             halves(pre.at[0, g], jnp.where(row == col, F32(1.0), F32(0.0)))
+        graduate(0, qs)
         fwd_wait(0)
-        graduate(0)
-        multiply(qb, take(mon, 0), take(pre, 7), t0s)
-        send_t0().start()
+        for g in range(2):
+            graduate(0, qs, [g])
+            t0s[g] = times(mon[0, g], pre[7, g])
+            send_t0(g).start()
         late[...] = mon[0]
 
     @pl.when(core == 1)
@@ -218,37 +251,46 @@
         copy_pre(0)
         for t in range(1, 5):
             multiply(pre.at[t], take(pre, t - 1), take(mon, t))
-        for t in range(5, 8):
+        for t in (5, 6):
             bwd_wait(t - 5)
             graduate(t)
             multiply(pre.at[t], take(pre, t - 1), take(mon, t))
-        send_t0().wait_recv()
-        for g in range(2):
-            halves(late.at[g], t0r[g])
-        pl.when(jnp.logical_not(last_chip))(
-            lambda: multiply(qb, lambda g: late[g], take(pre, 7), qs)
-        )
-
-    def chunk(j):
-        return lax.rem(z + nz + order[j], nz)
-
-    def chunk_rows(j):
-        return pl.ds(pl.multiple_of(chunk(j) * rows, rows), rows)
-
-    def carry_on(j, g, first=False):
-        src = qs.at[g, chunk_rows(j), :] if first else outc.at[j, g]
-        return remote(src, carry.at[j, g], cs_sem.at[j, g], cr_sem.at[j, g], tm + 2, co)
-
-    def carry_back(j, g):
-        return remote(carry.at[j, g], carry.at[j, g], cf_sem.at[j, g], cr_sem.at[j, g], tm - 1, co)
-
-    pieces = [(j, g) for j in range(nz) for g in range(2)]
+        graduate(7, t0s)
+
+        @pl.when(first_chip)
+        def _():
+            for g in range(2):
+                send_t0(g).wait_recv()
+                halves(late.at[g], t0r[g])
+            multiply(qb, take_late, take(pre, 6))
+            bwd_wait(2)
+            for g in range(2):
+                graduate(7, t0s, [g])
+                qs[g] = times(qb[g], mon[7, g])
+                for j in range(soon):
+                    carry_on(j, g, True).start()
+            for j in range(soon, nz):
+                for g in range(2):
+                    carry_on(j, g, True).start()
+            multiply(pre.at[7], take(pre, 6), take(mon, 7))
+
+        @pl.when(jnp.logical_not(first_chip))
+        def _():
+            bwd_wait(2)
+            graduate(7, t0s, [0, 1])
+            multiply(pre.at[7], take(pre, 6), take(mon, 7))
+            for g in range(2):
+                send_t0(g).wait_recv()
+                halves(late.at[g], t0r[g])
+
+                @pl.when(jnp.logical_not(last_chip))
+                def _():
+                    halves(qb.at[g], times(late[g], pre[7, g]))
 
     @pl.when(first_chip)
     def _():
         row = lax.broadcasted_iota(jnp.int32, (rows, n), 0)
         col = lax.broadcasted_iota(jnp.int32, (rows, n), 1)
-        pl.when(core == 1)(lambda: [carry_on(j, g, True).start() for j, g in pieces] and None)
         for j in range(nz):
             unit = jnp.where(row + chunk(j) * rows == col, F32(1.0), F32(0.0))
             for g in range(2):
@@ -430,7 +472,8 @@
     for i in range(3):
         pl.when(has_next)(lambda: fwd_halo(i).wait_send())
         pl.when(has_prev)(lambda: bwd_halo(i).wait_send())
-    pl.when(core == 0)(lambda: send_t0().wait_send())
+    for g in range(2):
+        pl.when(core == 0)(lambda: send_t0(g).wait_send())
     for j in range(nz):
         for g in range(2):
             pl.when((core == 1) & jnp.logical_not(last_chip))(lambda: carry_on(j, g).wait_send())
@@ -520,7 +563,7 @@
             pltpu.VMEM((ny - 1, 4, sub, n), F32),
             pltpu.VMEM((nz, ny - 1, 4, sub, n), F32),
             pltpu.VMEM((nz, 4, sub, n), F32),
-            dma((2,)), dma((8,)), dma((3,)), dma((3,)), dma((3,)), dma((3,)), dma((2,)),
+            dma((2,)), dma((8,)), dma((3,)), dma((3,)), dma((3,)), dma((3,)), dma((2, 2)),
             dma((nz, 2)), dma((nz, 2)), dma((nz, 2)),
             dma((2, half - 1, 4)), dma((2, half - 1, 4)), dma((2, 2)), dma((2, 2)),
             dma((2, half - 1)), dma((2, half - 1)), dma((2,)), dma((2,)),

time: 63.5 us -> 62.9 us (level)
    pallas_call x1, Pallas kernels: 60.7 us -> 60 us  [on_device(): pl.pallas_call(functools.partial(kernel, nz, ny), out_shape=(OUT(transiti...]
where the time goes in v4:
time: 62.9 us; the launch traced here: 62.8 us
  Pallas kernels  62.2 us (99%)
  between operations  0.64 us (1%)
    pallas_call x1, Pallas kernels, on_device(): pl.pallas_call(functools.partial(kernel, nz, ny), out_shape=(OUT(transiti...  60 us
    pallas_call x1, Pallas kernels, on_device(): pl.pallas_call(deliver, out_shape=(jax.ShapeDtypeStruct(cum.shape, F32),...  2.1 us

profile of v4, /device:TPU:6, one launch (start us, length us, event | category | flops | bytes accessed | tf_op | source)
XLA Modules:
  0.0 62.8 jit_solution(2278680865458495454)
XLA Ops:
  0.6 60.0 %shard_map.50 = (f32[8,2,256,256]{3,2,1,0:T(8,128)S(1)}, f32[8,8,256]{2,1,0:T(8,128)S(1)}) custom-call(f32[8,2,256,256]{3,2,1,0:T(8,128)} %trans.1, s32[2]{0:T(128)} %entry_in.1, f32[2]{0:T(128)} %share_in.1), custom_call_target="tpu_custom_call" | custom-call | flops 4630511616 | bytes 8388608 | tf_op jit(solution)/shard_map/pallas_call | solution.py:529
  60.7 2.1 %shard_map.51 = (f32[8,2,256,256]{3,2,1,0:T(8,128)}, f32[8,8,256]{2,1,0:T(8,128)}) custom-call(f32[8,2,256,256]{3,2,1,0:T(8,128)S(1)} %get-tuple-element.4.cum, f32[8,8,256]{2,1,0:T(8,128)S(1)} %get-tuple-element.5.pooled), custom_call_target="tpu_custom_call" | custom-call | tf_op jit(solution)/shard_map/pallas_call | solution.py:579

commit v5 on v4

--- a/solution.py
+++ b/solution.py
@@ -307,7 +307,7 @@
             carry_on(j, g).start()
             carry_back(j, g).start()
 
-    ahead = min(2 * nz, 2 * len(blocks[0]) + 4)
+    ahead = min(2 * nz, 2 * len(blocks[0]) + 6)
     pl.when(middle)(lambda: hand_on(pieces[:ahead]))
 
     def place(d, s):
@@ -431,6 +431,8 @@
             month(m, wa, m)
             return 0
 
+        if k == len(blocks) - 1 and half > 2:
+            a_stage(2, (0, 1))
         for h in range(2):
             if k == 0:
                 for m in (2 * h, 2 * h + 1):
@@ -444,8 +446,8 @@
             for j in block:
                 for o in range(1, ny):
                     yb_copy(j, h, o).start()
-            if k == len(blocks) - 1 and half > 2:
-                a_stage(2, (2 * h, 2 * h + 1))
+            if k == len(blocks) - 1 and half > 2 and h == 0:
+                a_stage(2, (2, 3))
         if k == 0 and ahead < 2 * nz:
             pl.when(middle)(lambda: hand_on(pieces[ahead:]))
         first += size

time: 62.9 us -> 62.2 us (0.989)
  Pallas kernels: 62.2 us -> 61.5 us
    pallas_call x1, Pallas kernels: 60 us -> 59.4 us  [on_device(): pl.pallas_call(functools.partial(kernel, nz, ny), out_shape=(OUT(transiti...]
where the time goes in v5:
time: 62.2 us; the launch traced here: 62.1 us
  Pallas kernels  61.5 us (99%)
  between operations  0.64 us (1%)
    pallas_call x1, Pallas kernels, on_device(): pl.pallas_call(functools.partial(kernel, nz, ny), out_shape=(OUT(transiti...  59.4 us
    pallas_call x1, Pallas kernels, on_device(): pl.pallas_call(deliver, out_shape=(jax.ShapeDtypeStruct(cum.shape, F32),...  2.1 us

profile of v5, /device:TPU:6, one launch (start us, length us, event | category | flops | bytes accessed | tf_op | source)
XLA Modules:
  0.0 62.1 jit_solution(7924207494564116631)
XLA Ops:
  0.6 59.4 %shard_map.50 = (f32[8,2,256,256]{3,2,1,0:T(8,128)S(1)}, f32[8,8,256]{2,1,0:T(8,128)S(1)}) custom-call(f32[8,2,256,256]{3,2,1,0:T(8,128)} %trans.1, s32[2]{0:T(128)} %entry_in.1, f32[2]{0:T(128)} %share_in.1), custom_call_target="tpu_custom_call" | custom-call | flops 4630511616 | bytes 8388608 | tf_op jit(solution)/shard_map/pallas_call | solution.py:531
  60.0 2.1 %shard_map.51 = (f32[8,2,256,256]{3,2,1,0:T(8,128)}, f32[8,8,256]{2,1,0:T(8,128)}) custom-call(f32[8,2,256,256]{3,2,1,0:T(8,128)S(1)} %get-tuple-element.4.cum, f32[8,8,256]{2,1,0:T(8,128)S(1)} %get-tuple-element.5.pooled), custom_call_target="tpu_custom_call" | custom-call | tf_op jit(solution)/shard_map/pallas_call | solution.py:581

commit v6 on v5

--- a/solution.py
+++ b/solution.py
@@ -74,22 +74,24 @@
             src_ref=src, dst_ref=dst, send_sem=ss, recv_sem=rs, device_id=(t, c), device_id_type=MESH
         )
 
-    def fwd_halo(i):
-        return remote(trans.at[5 + i], hp.at[i], fs_sem.at[i], hp_sem.at[i], tm + 1, co)
-
-    def bwd_halo(i):
-        return remote(trans.at[i], hn.at[i], bs_sem.at[i], hn_sem.at[i], tm - 1, co)
+    def fwd_halo(i, g):
+        return remote(trans.at[5 + i, g], hp.at[i, g], fs_sem.at[i, g], hp_sem.at[i, g], tm + 1, co)
+
+    def bwd_halo(i, g):
+        return remote(trans.at[i, g], hn.at[i, g], bs_sem.at[i, g], hn_sem.at[i, g], tm - 1, co)
 
     def own_copy(i):
         return pltpu.make_async_copy(trans.at[i], own.at[i], own_sem.at[i])
 
     def send_fwd():
         for i in (2, 1, 0):
-            fwd_halo(i).start()
+            for g in range(2):
+                fwd_halo(i, g).start()
 
     def send_bwd():
         for i in (0, 1, 2):
-            bwd_halo(i).start()
+            for g in range(2):
+                bwd_halo(i, g).start()
 
     pl.when((core == 0) & has_prev)(send_bwd)
     pl.when(has_next)(send_fwd)
@@ -179,11 +181,13 @@
     def copy_pre(t):
         pre[t] = mon[t]
 
-    def fwd_wait(i):
-        pl.when(has_prev)(lambda: fwd_halo(i).wait_recv())
-
-    def bwd_wait(i):
-        pl.when(has_next)(lambda: bwd_halo(i).wait_recv())
+    def fwd_wait(i, groups=(0, 1)):
+        for g in groups:
+            pl.when(has_prev)(lambda: fwd_halo(i, g).wait_recv())
+
+    def bwd_wait(i, groups=(0, 1)):
+        for g in groups:
+            pl.when(has_next)(lambda: bwd_halo(i, g).wait_recv())
 
     for copy in small:
         copy.wait()
@@ -236,8 +240,8 @@
         for g in range(2):
             halves(pre.at[0, g], jnp.where(row == col, F32(1.0), F32(0.0)))
         graduate(0, qs)
-        fwd_wait(0)
         for g in range(2):
+            fwd_wait(0, [g])
             graduate(0, qs, [g])
             t0s[g] = times(mon[0, g], pre[7, g])
             send_t0(g).start()
@@ -263,12 +267,16 @@
                 send_t0(g).wait_recv()
                 halves(late.at[g], t0r[g])
             multiply(qb, take_late, take(pre, 6))
-            bwd_wait(2)
-            for g in range(2):
-                graduate(7, t0s, [g])
-                qs[g] = times(qb[g], mon[7, g])
-                for j in range(soon):
-                    carry_on(j, g, True).start()
+            bwd_wait(2, [0])
+            graduate(7, t0s, [0])
+            qs[0] = times(qb[0], mon[7, 0])
+            bwd_wait(2, [1])
+            for j in range(soon):
+                carry_on(j, 0, True).start()
+            graduate(7, t0s, [1])
+            qs[1] = times(qb[1], mon[7, 1])
+            for j in range(soon):
+                carry_on(j, 1, True).start()
             for j in range(soon, nz):
                 for g in range(2):
                     carry_on(j, g, True).start()
@@ -276,9 +284,10 @@
 
         @pl.when(jnp.logical_not(first_chip))
         def _():
-            bwd_wait(2)
-            graduate(7, t0s, [0, 1])
-            multiply(pre.at[7], take(pre, 6), take(mon, 7))
+            for g in range(2):
+                bwd_wait(2, [g])
+                graduate(7, t0s, [g])
+                halves(pre.at[7, g], times(pre[6, g], mon[7, g]))
             for g in range(2):
                 send_t0(g).wait_recv()
                 halves(late.at[g], t0r[g])
@@ -307,7 +316,7 @@
             carry_on(j, g).start()
             carry_back(j, g).start()
 
-    ahead = min(2 * nz, 2 * len(blocks[0]) + 6)
+    ahead = min(2 * nz, 2 * len(blocks[0]) + 10)
     pl.when(middle)(lambda: hand_on(pieces[:ahead]))
 
     def place(d, s):
@@ -448,6 +457,7 @@
                     yb_copy(j, h, o).start()
             if k == len(blocks) - 1 and half > 2 and h == 0:
                 a_stage(2, (2, 3))
+                b_stage(1)
         if k == 0 and ahead < 2 * nz:
             pl.when(middle)(lambda: hand_on(pieces[ahead:]))
         first += size
@@ -455,7 +465,7 @@
     for s in range(1, half - 1):
         if s > 1:
             a_stage(s + 1)
-        b_stage(s)
+            b_stage(s)
 
     own_at = nz - 1
     for m in range(4):
@@ -472,8 +482,9 @@
         ya_copy(o).start()
     b_stage(half - 1)
     for i in range(3):
-        pl.when(has_next)(lambda: fwd_halo(i).wait_send())
-        pl.when(has_prev)(lambda: bwd_halo(i).wait_send())
+        for g in range(2):
+            pl.when(has_next)(lambda: fwd_halo(i, g).wait_send())
+            pl.when(has_prev)(lambda: bwd_halo(i, g).wait_send())
     for g in range(2):
         pl.when(core == 0)(lambda: send_t0(g).wait_send())
     for j in range(nz):
@@ -565,7 +576,7 @@
             pltpu.VMEM((ny - 1, 4, sub, n), F32),
             pltpu.VMEM((nz, ny - 1, 4, sub, n), F32),
             pltpu.VMEM((nz, 4, sub, n), F32),
-            dma((2,)), dma((8,)), dma((3,)), dma((3,)), dma((3,)), dma((3,)), dma((2, 2)),
+            dma((2,)), dma((8,)), dma((3, 2)), dma((3, 2)), dma((3, 2)), dma((3, 2)), dma((2, 2)),
             dma((nz, 2)), dma((nz, 2)), dma((nz, 2)),
             dma((2, half - 1, 4)), dma((2, half - 1, 4)), dma((2, 2)), dma((2, 2)),
             dma((2, half - 1)), dma((2, half - 1)), dma((2,)), dma((2,)),

time: 62.2 us -> 61.4 us (0.987)
  Pallas kernels: 61.5 us -> 60.7 us
    pallas_call x1, Pallas kernels: 59.4 us -> 58.6 us  [on_device(): pl.pallas_call(functools.partial(kernel, nz, ny), out_shape=(OUT(transiti...]
where the time goes in v6:
time: 61.4 us; the launch traced here: 61.3 us
  Pallas kernels  60.7 us (99%)
  between operations  0.64 us (1%)
    pallas_call x1, Pallas kernels, on_device(): pl.pallas_call(functools.partial(kernel, nz, ny), out_shape=(OUT(transiti...  58.6 us
    pallas_call x1, Pallas kernels, on_device(): pl.pallas_call(deliver, out_shape=(jax.ShapeDtypeStruct(cum.shape, F32),...  2.1 us

profile of v6, /device:TPU:6, one launch (start us, length us, event | category | flops | bytes accessed | tf_op | source)
XLA Modules:
  0.0 61.3 jit_solution(3036498759286599553)
XLA Ops:
  0.6 58.6 %shard_map.50 = (f32[8,2,256,256]{3,2,1,0:T(8,128)S(1)}, f32[8,8,256]{2,1,0:T(8,128)S(1)}) custom-call(f32[8,2,256,256]{3,2,1,0:T(8,128)} %trans.1, s32[2]{0:T(128)} %entry_in.1, f32[2]{0:T(128)} %share_in.1), custom_call_target="tpu_custom_call" | custom-call | flops 4630511616 | bytes 8388608 | tf_op jit(solution)/shard_map/pallas_call | solution.py:542
  59.2 2.1 %shard_map.51 = (f32[8,2,256,256]{3,2,1,0:T(8,128)}, f32[8,8,256]{2,1,0:T(8,128)}) custom-call(f32[8,2,256,256]{3,2,1,0:T(8,128)S(1)} %get-tuple-element.4.cum, f32[8,8,256]{2,1,0:T(8,128)S(1)} %get-tuple-element.5.pooled), custom_call_target="tpu_custom_call" | custom-call | tf_op jit(solution)/shard_map/pallas_call | solution.py:592
